TPU v7x, 768 devices: a whole 4x8x12 slice. The times are simulated.
768 devices in a mesh: dp: 64 (over z_lo, y, core), tensor: 12 (over z_hi, x).
Axes of the slice: x: 4, y: 8, z: 12 (z_hi: 3, z_lo: 4; z = z_hi * 4 + z_lo), core: 2. Of those that a mesh axis runs over, the one named last changes fastest.
Arguments:
- gate_pre: bfloat16 [24576, 1792], P(('dp', 'tensor')), parts along dimension 0, may hold values from -6 to 6
- up_pre: bfloat16 [24576, 1792], P(('dp', 'tensor')), parts along dimension 0, may hold values from -6 to 6
- down_weight: bfloat16 [1792, 6144], P(None, 'tensor'), may hold values from -0.125 to 0.125
- out_grad: bfloat16 [24576, 6144], P(('dp', 'tensor')), parts along dimension 0, may hold values from -6 to 6
Outputs:
- output: bfloat16 [24576, 6144], P(('dp', 'tensor')), parts along dimension 0
- gate_grad: bfloat16 [24576, 1792], P(('dp', 'tensor')), parts along dimension 0
- up_grad: bfloat16 [24576, 1792], P(('dp', 'tensor')), parts along dimension 0
- weight_grad: bfloat16 [1792, 393216], P(None, ('dp', 'tensor')), parts along dimension 1
There are 64 independent parts, one for each index of `dp`. A program takes and returns all parts, laid end to end along the dimension named above; an argument that names none is the same for every part. Nothing has to cross between parts.
All inputs are finite; a program needn't handle non-finite values.
Results may differ from a plain program's by a relative error of at most 0.034.
Values may be sent and summed in bfloat16 or wider, within the bound.
No kernel may reach another device: no remote copies, remote signals or barrier semaphores. Data moves between devices by JAX's collectives and lax.ppermute only.
A program may use at most 32 MiB of HBM per device.

v0:
```python
import jax
import jax.numpy as jnp
from jax import lax
from jax.sharding import PartitionSpec as P


def grad_product(block_rows, cotangent):
    return lax.dot_general(
        block_rows, cotangent, (((0,), (0,)), ((), ())), preferred_element_type=jnp.float32
    )


def forward_pass(hidden, down_weight):
    columns = jnp.dot(
        lax.all_gather(hidden, "tensor", axis=0, tiled=True),
        down_weight,
        preferred_element_type=jnp.float32,
    )
    return lax.all_to_all(
        columns.astype(jnp.bfloat16), "tensor", split_axis=0, concat_axis=1, tiled=True
    )


def backward_pass(hidden, down_weight, out_grad):
    cotangent = lax.all_to_all(out_grad, "tensor", split_axis=1, concat_axis=0, tiled=True)
    weight_sum = grad_product(lax.all_gather(hidden, "tensor", axis=0, tiled=True), cotangent)
    hidden_grad = lax.psum_scatter(
        lax.dot_general(
            cotangent, down_weight, (((1,), (1,)), ((), ())), preferred_element_type=jnp.float32
        ).astype(jnp.bfloat16),
        "tensor",
        scatter_dimension=0,
        tiled=True,
    ).astype(jnp.float32)
    return (hidden_grad, weight_sum)


def body(gate_pre, up_pre, down_weight, out_grad):
    gate_vals = gate_pre.astype(jnp.float32)
    up_vals = up_pre.astype(jnp.float32)
    sig = jax.nn.sigmoid(gate_vals)
    act = gate_vals * sig
    hidden = (act * up_vals).astype(jnp.bfloat16)
    output = forward_pass(hidden, down_weight)
    hidden_grad, weight_sum = backward_pass(hidden, down_weight, out_grad)
    gate_grad = (hidden_grad * up_vals * sig * (1.0 + gate_vals * (1.0 - sig))).astype(jnp.bfloat16)
    up_grad = (hidden_grad * act).astype(jnp.bfloat16)
    weight_grad = weight_sum.astype(jnp.bfloat16)
    return (output, gate_grad, up_grad, weight_grad)


def solution(mesh):
    return jax.shard_map(
        body,
        mesh=mesh,
        in_specs=(
            P(("dp", "tensor"), None),
            P(("dp", "tensor"), None),
            P(None, "tensor"),
            P(("dp", "tensor"), None),
        ),
        out_specs=(
            P(("dp", "tensor"), None),
            P(("dp", "tensor"), None),
            P(("dp", "tensor"), None),
            P(None, ("dp", "tensor")),
        ),
        check_vma=False,
    )
```

profile of v0, /device:TPU:6, one launch (start us, length us, event | category | flops | bytes accessed | tf_op | source)
XLA Modules:
  0.0 332.1 jit_solution(17394659095823340777)
XLA Ops:
  7.2 0.0 copy-start
  7.2 0.0 reduce-scatter.2.cloned.1.call-start
  7.2 1.1 copy.16
  8.4 31.9 %all_to_all.38 = bf16[32,12,512]{2,0,1:T(8,128)(2,1)S(1)} all-to-all(bf16[32,12,512]{2,0,1:T(8,128)(2,1)S(1)} %bitcast.18), channel_id=1, replica_groups=mesh['dp'=64,'tensor'=12] {'tensor'}, dimensions={1} | all-to-all | bytes 786432 | tf_op jit(solution)/shard_map/all_to_all | solution.py:25
  40.3 0.0 copy-done
  40.3 0.0 copy-start.1
  40.3 0.0 copy-start.2
  40.3 2.0 convolution_convert_fusion.1
  42.3 0.0 reduce-scatter.2.cloned.1.call-update
  42.3 0.0 all-gather.2.cloned.1.call-start
  42.3 173.8 %reduce-scatter.2.cloned.1.call-done = bf16[32,1792]{1,0:T(8,128)(2,1)} async-done(((bf16[384,1792]{1,0:T(8,128)(2,1)}), bf16[32,1792]{1,0:T(8,128)(2,1)}) %reduce-scatter.2.cloned.1.call-update) | async-done | bytes 114704 | tf_op jit(solution)/shard_map/reduce_scatter | solution.py:27
  216.1 0.0 copy-done.1
  216.1 0.0 copy-done.2
  216.1 1.7 fusion.4
  217.9 0.0 all-gather.2.cloned.1.call-update
  217.9 81.8 %all-gather.2.cloned.1.call-done = bf16[384,1792]{1,0:T(8,128)(2,1)} async-done(((bf16[32,1792]{1,0:T(8,128)(2,1)}), bf16[384,1792]{1,0:T(8,128)(2,1)}) %all-gather.2.cloned.1.call-update) | async-done | bytes 1376272 | tf_op jit(solution)/shard_map/all_gather | solution.py:15
  299.7 3.0 convolution_convert_fusion.2
  302.6 8.5 %all-to-all-start = ((bf16[12,32,512]{2,1,0:T(8,128)(2,1)}), bf16[12,32,512]{2,1,0:T(8,128)(2,1)S(1)}, u32[]{:S(2)}, u32[]{:S(2)}) async-start(bf16[12,32,512]{2,1,0:T(8,128)(2,1)} %bitcast), calls=%async_computation | async-start | bytes 786432 | tf_op jit(solution)/shard_map/all_to_all | solution.py:19
  311.1 3.7 %convolution_convert_fusion = bf16[1792,512]{1,0:T(8,128)(2,1)} fusion(bf16[384,1792]{1,0:T(8,128)(2,1)} %all-gather.2.cloned.1.call-done, bf16[384,512]{1,0:T(8,128)(2,1)S(1)} %bitcast.21), kind=kOutput, calls=%fused_computation | convolution fusion | flops 705560576 | bytes 3604480 | tf_op jit(solution)/shard_map/dot_general | solution.py:8
  314.8 9.7 %all-to-all-done = bf16[12,32,512]{2,1,0:T(8,128)(2,1)S(1)} async-done(((bf16[12,32,512]{2,1,0:T(8,128)(2,1)}), bf16[12,32,512]{2,1,0:T(8,128)(2,1)S(1)}, u32[]{:S(2)}, u32[]{:S(2)}) %all-to-all-start) | async-done | bytes 393248 | tf_op jit(solution)/shard_map/all_to_all | solution.py:19
  324.5 0.8 copy.14
Async XLA Ops:
  7.2 33.1 %copy-start = (bf16[1792,512]{1,0:T(8,128)(2,1)S(1)}, bf16[1792,512]{1,0:T(8,128)(2,1)}, u32[]{:S(2)}) copy-start(bf16[1792,512]{1,0:T(8,128)(2,1)} %param.6) | copy-start | bytes 5505028
  7.2 208.9 %reduce-scatter.2.cloned.1.call-start = ((), (), s32[]{:S(2)}) async-start(), calls=%async_computation.4 | async-start | bytes 1490944 | tf_op jit(solution)/shard_map/reduce_scatter | solution.py:27
  40.3 175.9 %copy-start.1 = (bf16[32,1792]{1,0:T(8,128)(2,1)S(1)}, bf16[32,1792]{1,0:T(8,128)(2,1)}, u32[]{:S(2)}) copy-start(bf16[32,1792]{1,0:T(8,128)(2,1)} %param.4) | copy-start | bytes 344068
  40.3 175.9 %copy-start.2 = (bf16[32,1792]{1,0:T(8,128)(2,1)S(1)}, bf16[32,1792]{1,0:T(8,128)(2,1)}, u32[]{:S(2)}) copy-start(bf16[32,1792]{1,0:T(8,128)(2,1)} %param.5) | copy-start | bytes 344068
  42.3 257.4 %all-gather.2.cloned.1.call-start = ((), (), s32[]{:S(2)}) async-start(), calls=%async_computation.3 | async-start | bytes 1490944 | tf_op jit(solution)/shard_map/all_gather | solution.py:15
  302.6 21.9 %all-to-all-start = ((bf16[12,32,512]{2,1,0:T(8,128)(2,1)}), bf16[12,32,512]{2,1,0:T(8,128)(2,1)S(1)}, u32[]{:S(2)}, u32[]{:S(2)}) async-start(bf16[12,32,512]{2,1,0:T(8,128)(2,1)} %bitcast), calls=%async_computation | async-start | bytes 786432 | tf_op jit(solution)/shard_map/all_to_all | solution.py:19
Sparse Core Ops, SparseCore 0:
  42.4 173.6 reduce-scatter.1
  221.4 78.2 all-gather.1
where the time goes:
time: 335 us; the launch traced here: 332 us
  waiting for transfers between devices  265 us (79%)
  blocking collectives  31.9 us (10%)
  between operations  14.1 us (4%)
  matrix products  8.66 us (3%)
  starting transfers between devices  8.55 us (3%)
    reduce_scatter x1, waiting for transfers between devices, backward_pass(): lax.psum_scatter(lax.dot_general(cotangent, down_weight, (((1,), (1,)), (...  174 us
    all_gather x1, waiting for transfers between devices, forward_pass(): lax.all_gather(hidden, 'tensor', axis=0, tiled=True)  81.8 us
    all_to_all x1, blocking collectives, backward_pass(): lax.all_to_all(out_grad, 'tensor', split_axis=1, concat_axis=0, tiled=True)  31.9 us
    all_to_all x1, waiting for transfers between devices, forward_pass(): lax.all_to_all(columns.astype(jnp.bfloat16), 'tensor', split_axis=0, conc...  9.68 us
    all_to_all x1, starting transfers between devices, forward_pass(): lax.all_to_all(columns.astype(jnp.bfloat16), 'tensor', split_axis=0, conc...  8.47 us
  transfers between devices with their start and end apart: 3, of which 3 were waited for; matrix products, arithmetic and copies ran while one was open for 1% of the time, Pallas kernels for 0%

commit v1 on v0

v1 whole, which is shorter than its diff:
```python
import jax
import jax.numpy as jnp
from jax import lax
from jax.sharding import PartitionSpec as P


def grad_product(block_rows, cotangent):
    return lax.dot_general(
        block_rows, cotangent, (((0,), (0,)), ((), ())), preferred_element_type=jnp.float32
    )


def body(gate_pre, up_pre, down_weight, out_grad):
    rows, hidden_width = gate_pre.shape
    width = down_weight.shape[1]
    group = out_grad.shape[1] // width
    gate_vals = gate_pre.astype(jnp.float32)
    up_vals = up_pre.astype(jnp.float32)
    sig = jax.nn.sigmoid(gate_vals)
    act = gate_vals * sig
    hidden = (act * up_vals).astype(jnp.bfloat16)

    cotangent_blocks = jnp.swapaxes(out_grad.reshape(rows, group, width), 0, 1)
    hidden_copies = jnp.broadcast_to(hidden[None], (group, rows, hidden_width))
    sent = jnp.concatenate([cotangent_blocks, hidden_copies], axis=2)
    got = lax.all_to_all(sent, "tensor", 0, 0, tiled=True)
    got = got.reshape(group * rows, width + hidden_width)
    cotangent = got[:, :width]
    hidden_all = got[:, width:]

    columns = jnp.dot(hidden_all, down_weight, preferred_element_type=jnp.float32)
    partial_sums = lax.dot_general(
        cotangent, down_weight, (((1,), (1,)), ((), ())), preferred_element_type=jnp.float32
    )
    back = jnp.concatenate(
        [columns.astype(jnp.bfloat16), partial_sums.astype(jnp.bfloat16)], axis=1
    ).reshape(group, rows, width + hidden_width)
    mine = lax.all_to_all(back, "tensor", 0, 0, tiled=True)
    output = jnp.swapaxes(mine[:, :, :width], 0, 1).reshape(rows, group * width)
    hidden_grad = jnp.sum(mine[:, :, width:].astype(jnp.float32), axis=0)

    weight_grad = grad_product(hidden_all, cotangent).astype(jnp.bfloat16)
    gate_grad = (hidden_grad * up_vals * sig * (1.0 + gate_vals * (1.0 - sig))).astype(jnp.bfloat16)
    up_grad = (hidden_grad * act).astype(jnp.bfloat16)
    return (output, gate_grad, up_grad, weight_grad)


def solution(mesh):
    return jax.shard_map(
        body,
        mesh=mesh,
        in_specs=(
            P(("dp", "tensor"), None),
            P(("dp", "tensor"), None),
            P(None, "tensor"),
            P(("dp", "tensor"), None),
        ),
        out_specs=(
            P(("dp", "tensor"), None),
            P(("dp", "tensor"), None),
            P(("dp", "tensor"), None),
            P(None, ("dp", "tensor")),
        ),
        check_vma=False,
    )
```

time: 335 us -> 143 us (0.43)
  waiting for transfers between devices: 265 us -> 48.5 us
  blocking collectives: 31.9 us -> 69.3 us
  between operations: 14.1 us -> 0.73 us
    reduce_scatter x1 -> x0, waiting for transfers between devices: 174 us -> none  [backward_pass(): lax.psum_scatter(lax.dot_general(cotangent, down_weight, (((1,), (1,)), (...]
    all_gather x1 -> x0, waiting for transfers between devices: 81.8 us -> none  [forward_pass(): lax.all_gather(hidden, 'tensor', axis=0, tiled=True)]
    all_to_all x1, waiting for transfers between devices: 9.68 us -> 48.5 us  [body(): mine = lax.all_to_all(back, 'tensor', 0, 0, tiled=True)]
    all_to_all x1, blocking collectives: 31.9 us -> 69.3 us  [body(): got = lax.all_to_all(sent, 'tensor', 0, 0, tiled=True)]
  transfers between devices with their start and end apart: 3 -> 1, of which waited for: 3 -> 1; matrix products, arithmetic and copies ran while one was open for 1% -> 3% of each run, Pallas kernels for 0% -> 0%
where the time goes in v1:
time: 143 us
  blocking collectives  69.3 us (48%)
  waiting for transfers between devices  48.5 us (34%)
  starting transfers between devices  10.8 us (8%)
  matrix products  5.55 us (4%)
  local copies, waits for them, and re-layouts  3.88 us (3%)
  other arithmetic  3.86 us (3%)
    all_to_all x1, blocking collectives, body(): got = lax.all_to_all(sent, 'tensor', 0, 0, tiled=True)  69.3 us
    all_to_all x1, waiting for transfers between devices, body(): mine = lax.all_to_all(back, 'tensor', 0, 0, tiled=True)  48.5 us
    all_to_all x1, starting transfers between devices, body(): mine = lax.all_to_all(back, 'tensor', 0, 0, tiled=True)  10.8 us
    dot_general x1, matrix products, grad_product(): lax.dot_general(block_rows, cotangent, (((0,), (0,)), ((), ())), preferre...  3.78 us
  transfers between devices with their start and end apart: 1, of which 1 were waited for; matrix products, arithmetic and copies ran while one was open for 3% of the time, Pallas kernels for 0%

profile of v1, /device:TPU:6, one launch (start us, length us, event | category | flops | bytes accessed | tf_op | source)
XLA Modules:
  0.0 142.6 jit_solution(7995621453459811388)
XLA Ops:
  0.6 0.0 copy-start
  0.6 0.0 copy-start.3
  0.7 0.0 copy-start.2
  0.7 1.4 reshape.21
  2.1 0.2 copy.12
  2.3 0.0 copy-done.3
  2.3 0.0 copy-done.2
  2.3 0.1 fusion.4
  2.4 0.1 broadcast_in_dim.2
  2.5 0.1 pad_maximum_fusion
  2.7 69.3 %all_to_all.10 = bf16[12,32,2304]{2,1,0:T(8,128)(2,1)S(1)} all-to-all(bf16[12,32,2304]{2,1,0:T(8,128)(2,1)S(1)} %pad_maximum_fusion), channel_id=1, replica_groups=mesh['dp'=64,'tensor'=12] {'tensor'}, dimensions={0} | all-to-all | bytes 3538944 | tf_op jit(solution)/shard_map/all_to_all | solution.py:26
  72.0 0.0 copy-start.1
  72.0 0.0 copy-done
  72.0 0.9 convolution_convert_fusion.1
  72.9 0.3 copy-done.1
  73.2 0.9 convolution_convert_fusion.2
  74.1 1.3 pad_maximum_fusion.1
  75.4 10.8 %all-to-all-start.1 = ((bf16[12,32,2304]{2,1,0:T(8,128)(2,1)}), bf16[12,32,2304]{2,1,0:T(8,128)(2,1)}, u32[]{:S(2)}, u32[]{:S(2)}) async-start(bf16[12,32,2304]{2,1,0:T(8,128)(2,1)} %bitcast.9), calls=%async_computation.1 | async-start | bytes 3538944 | tf_op jit(solution)/shard_map/all_to_all | solution.py:38
  86.2 3.8 %convolution_convert_fusion = bf16[1792,512]{1,0:T(8,128)(2,1)} fusion(bf16[384,2304]{1,0:T(8,128)(2,1)} %bitcast.13), kind=kOutput, calls=%fused_computation | convolution fusion | flops 705560576 | bytes 3604480 | tf_op jit(solution)/shard_map/dot_general | solution.py:8
  90.0 48.5 %all-to-all-done.1 = bf16[12,32,2304]{2,1,0:T(8,128)(2,1)} async-done(((bf16[12,32,2304]{2,1,0:T(8,128)(2,1)}), bf16[12,32,2304]{2,1,0:T(8,128)(2,1)}, u32[]{:S(2)}, u32[]{:S(2)}) %all-to-all-start.1) | async-done | bytes 1769504 | tf_op jit(solution)/shard_map/all_to_all | solution.py:38
  138.5 1.5 %convert_reduce_fusion = f32[32,1792]{1,0:T(8,128)S(1)} fusion(bf16[12,32,2304]{2,1,0:T(8,128)(2,1)} %all-to-all-done.1), kind=kLoop, calls=%fused_computation.2 | loop fusion | flops 1318912 | bytes 1605632 | tf_op jit(solution)/shard_map/reduce_sum | solution.py:40
  140.0 0.8 multiply_convert_fusion
  140.8 1.0 slice_bitcast_fusion
  141.9 0.8 copy.14
Async XLA Ops:
  0.6 71.4 %copy-start = (bf16[1792,512]{1,0:T(8,128)(2,1)S(1)}, bf16[1792,512]{1,0:T(8,128)(2,1)}, u32[]{:S(2)}) copy-start(bf16[1792,512]{1,0:T(8,128)(2,1)} %param.6) | copy-start | bytes 5505028
  0.6 1.7 %copy-start.3 = (bf16[32,1792]{1,0:T(8,128)(2,1)S(1)}, bf16[32,1792]{1,0:T(8,128)(2,1)}, u32[]{:S(2)}) copy-start(bf16[32,1792]{1,0:T(8,128)(2,1)} %param.4) | copy-start | bytes 344068
  0.7 1.7 %copy-start.2 = (bf16[32,1792]{1,0:T(8,128)(2,1)S(1)}, bf16[32,1792]{1,0:T(8,128)(2,1)}, u32[]{:S(2)}) copy-start(bf16[32,1792]{1,0:T(8,128)(2,1)} %param.5) | copy-start | bytes 344068
  72.0 1.2 copy-start.1
  75.4 63.1 %all-to-all-start.1 = ((bf16[12,32,2304]{2,1,0:T(8,128)(2,1)}), bf16[12,32,2304]{2,1,0:T(8,128)(2,1)}, u32[]{:S(2)}, u32[]{:S(2)}) async-start(bf16[12,32,2304]{2,1,0:T(8,128)(2,1)} %bitcast.9), calls=%async_computation.1 | async-start | bytes 3538944 | tf_op jit(solution)/shard_map/all_to_all | solution.py:38

commit v2 on v1

v2 whole, which is shorter than its diff:
```python
import jax
import jax.numpy as jnp
from jax import lax
from jax.sharding import Mesh, PartitionSpec as P

PLANES = 3
GROUP = ("plane", "line")


def shift(value, axis, size, step):
    return lax.ppermute(value, axis, [(i, (i + step) % size) for i in range(size)])


def body(gate_pre, up_pre, down_weight, out_grad):
    rows, hidden_width = gate_pre.shape
    width = down_weight.shape[1]
    group = out_grad.shape[1] // width
    line = group // PLANES
    my_plane, my_line = lax.axis_index("plane"), lax.axis_index("line")

    gate_vals = gate_pre.astype(jnp.float32)
    up_vals = up_pre.astype(jnp.float32)
    sig = jax.nn.sigmoid(gate_vals)
    act = gate_vals * sig
    hidden = (act * up_vals).astype(jnp.bfloat16)

    by_plane = [hidden] + [shift(hidden, "plane", PLANES, -j) for j in range(1, PLANES)]

    blocks = jnp.swapaxes(out_grad.reshape(rows, group, width), 0, 1)
    cotangent = lax.all_to_all(blocks, GROUP, 0, 0, tiled=True)
    cotangent = cotangent.reshape(PLANES, line, rows, width)
    cotangent = jnp.roll(cotangent, (-my_plane, -my_line), (0, 1))
    cotangent = jnp.swapaxes(cotangent, 0, 1).reshape(group * rows, width)

    mine = jnp.concatenate(by_plane, axis=0)
    by_line = [mine] + [shift(mine, "line", line, -k) for k in range(1, line)]
    hidden_all = jnp.concatenate(by_line, axis=0)

    partial_sums = lax.dot_general(
        cotangent, down_weight, (((1,), (1,)), ((), ())), preferred_element_type=jnp.float32
    ).astype(jnp.bfloat16).reshape(line, PLANES * rows, hidden_width)
    line_sums = [partial_sums[0]] + [
        shift(partial_sums[k], "line", line, k) for k in range(1, line)
    ]
    line_sum = sum(s.astype(jnp.float32) for s in line_sums)
    line_sum = line_sum.astype(jnp.bfloat16).reshape(PLANES, rows, hidden_width)
    plane_sums = [line_sum[0]] + [
        shift(line_sum[j], "plane", PLANES, j) for j in range(1, PLANES)
    ]
    hidden_grad = sum(s.astype(jnp.float32) for s in plane_sums)

    columns = jnp.dot(hidden_all, down_weight, preferred_element_type=jnp.float32)
    columns = columns.astype(jnp.bfloat16).reshape(line, PLANES, rows, width)
    columns = jnp.roll(columns, (my_line, my_plane), (0, 1))
    columns = jnp.swapaxes(columns, 0, 1).reshape(group, rows, width)
    output = lax.all_to_all(columns, GROUP, 0, 0, tiled=True)
    output = jnp.swapaxes(output, 0, 1).reshape(rows, group * width)

    weight_grad = lax.dot_general(
        hidden_all, cotangent, (((0,), (0,)), ((), ())), preferred_element_type=jnp.float32
    ).astype(jnp.bfloat16)
    gate_grad = (hidden_grad * up_vals * sig * (1.0 + gate_vals * (1.0 - sig))).astype(jnp.bfloat16)
    up_grad = (hidden_grad * act).astype(jnp.bfloat16)
    return (output, gate_grad, up_grad, weight_grad)


def solution(mesh):
    tokens = ("dp",) + GROUP
    fine = Mesh(mesh.devices.reshape(mesh.shape["dp"], PLANES, -1), tokens)
    return jax.shard_map(
        body,
        mesh=fine,
        in_specs=(P(tokens, None), P(tokens, None), P(None, GROUP), P(tokens, None)),
        out_specs=(P(tokens, None), P(tokens, None), P(tokens, None), P(None, tokens)),
        check_vma=False,
    )
```

time: 143 us -> 111 us (0.78)
  blocking collectives: 69.3 us -> 0 us
  starting transfers between devices: 10.8 us -> 68 us
  waiting for transfers between devices: 48.5 us -> 23.3 us
  local copies, waits for them, and re-layouts: 3.88 us -> 9.81 us
    all_to_all x1 -> x0, blocking collectives: 69.3 us -> none  [body(): got = lax.all_to_all(sent, 'tensor', 0, 0, tiled=True)]
    all_to_all x1 -> x2, waiting for transfers between devices: 48.5 us -> 0.01 us  [the longest x1 0.01 us: body(): cotangent = lax.all_to_all(blocks, GROUP, 0, 0, tiled=True)]
    ppermute x0 -> x10, starting transfers between devices: none -> 46.9 us  [shift(): lax.ppermute(value, axis, [(i, (i + step) % size) for i in range(size)])]
    ppermute x0 -> x10, waiting for transfers between devices: none -> 23.3 us  [shift(): lax.ppermute(value, axis, [(i, (i + step) % size) for i in range(size)])]
    all_to_all x1 -> x2, starting transfers between devices: 10.8 us -> 21 us  [the longest x1 10.9 us: body(): output = lax.all_to_all(columns, GROUP, 0, 0, tiled=True)]
    unnamed x9 -> x19, local copies, waits for them, and re-layouts: 1.35 us -> 4.35 us
    unnamed x0 -> x1, other arithmetic: none -> 1.81 us
    slice x0 -> x2, local copies, waits for them, and re-layouts: none -> 1.67 us  [the longest x1 1 us: body(): partial_sums[k]]
  transfers between devices with their start and end apart: 1 -> 12, of which waited for: 1 -> 6; matrix products, arithmetic and copies ran while one was open for 3% -> 12% of each run, Pallas kernels for 0% -> 0%
where the time goes in v2:
time: 111 us
  starting transfers between devices  68 us (61%)
  waiting for transfers between devices  23.3 us (21%)
  local copies, waits for them, and re-layouts  9.81 us (9%)
  other arithmetic  4.65 us (4%)
  matrix products  4.15 us (4%)
    ppermute x10, starting transfers between devices, shift(): lax.ppermute(value, axis, [(i, (i + step) % size) for i in range(size)])  46.9 us
    ppermute x10, waiting for transfers between devices, shift(): lax.ppermute(value, axis, [(i, (i + step) % size) for i in range(size)])  23.3 us
    all_to_all x1, starting transfers between devices, body(): output = lax.all_to_all(columns, GROUP, 0, 0, tiled=True)  10.9 us
    all_to_all x1, starting transfers between devices, body(): cotangent = lax.all_to_all(blocks, GROUP, 0, 0, tiled=True)  10.1 us
    unnamed x19, local copies, waits for them, and re-layouts  4.35 us
    dot_general x1, matrix products, body(): lax.dot_general(hidden_all, cotangent, (((0,), (0,)), ((), ())), preferre...  2.37 us
  transfers between devices with their start and end apart: 12, of which 6 were waited for; matrix products, arithmetic and copies ran while one was open for 12% of the time, Pallas kernels for 0%

profile of v2, /device:TPU:6, one launch (start us, length us, event | category | flops | bytes accessed | tf_op | source)
XLA Modules:
  0.0 110.8 jit_solution(15189705848451148922)
XLA Ops:
  0.6 0.0 copy-start
  0.6 1.8 %constant_dynamic-update-slice_fusion.5 = (bf16[384,1792]{1,0:T(8,128)(2,1)}, bf16[32,1792]{1,0:T(8,128)(2,1)S(1)}) fusion(bf16[32,1792]{1,0:T(8,128)(2,1)} %param.5, bf16[32,1792]{1,0:T(8,128)(2,1)} %param.4), kind=kLoop, calls=%fused_computation.38 | loop fusion | flops 458751 | bytes 458752
  2.5 14.5 %collective-permute-start = (bf16[32,1792]{1,0:T(8,128)(2,1)S(1)}, bf16[32,1792]{1,0:T(8,128)(2,1)S(1)}, u32[]{:S(2)}, u32[]{:S(2)}) collective-permute-start(bf16[32,1792]{1,0:T(8,128)(2,1)S(1)} %get-tuple-element.5), channel_id=1, source_target_pairs={{0,8},{4,0},{8,4},{1,9},{5,1},{9,5},{2,10},{6,2},{10,6},{3,11},{7,... | collective-permute-start | bytes 344072 | tf_op jit(solution)/shard_map/ppermute | solution.py:11
  17.0 1.9 %collective-permute-start.1 = (bf16[32,1792]{1,0:T(8,128)(2,1)S(1)}, bf16[32,1792]{1,0:T(8,128)(2,1)S(1)}, u32[]{:S(2)}, u32[]{:S(2)}) collective-permute-start(bf16[32,1792]{1,0:T(8,128)(2,1)S(1)} %get-tuple-element.5), channel_id=1, source_target_pairs={{0,4},{4,8},{8,0},{1,5},{5,9},{9,1},{2,6},{6,10},{10,2},{3,7},{7,1... | collective-permute-start | bytes 344072 | tf_op jit(solution)/shard_map/ppermute | solution.py:11
  18.9 1.3 %reshape.45 = bf16[32,12,512]{2,1,0:T(8,128)(2,1)S(1)} reshape(bf16[32,6144]{1,0:T(8,128)(2,1)} %param.7) | data formatting | bytes 786432 | tf_op jit(solution)/shard_map/reshape | solution.py:29
  20.2 1.0 copy.16
  21.2 10.1 %all-to-all-start.1 = ((bf16[12,32,512]{2,1,0:T(8,128)(2,1)}), bf16[12,32,512]{2,1,0:T(8,128)(2,1)S(1)}, u32[]{:S(2)}, u32[]{:S(2)}) async-start(bf16[12,32,512]{2,1,0:T(8,128)(2,1)} %copy.16), calls=%async_computation.1 | async-start | bytes 786432 | tf_op jit(solution)/shard_map/all_to_all | solution.py:30
  31.3 0.0 collective-permute-done
  31.3 3.5 %collective-permute-done.1 = bf16[32,1792]{1,0:T(8,128)(2,1)S(1)} collective-permute-done((bf16[32,1792]{1,0:T(8,128)(2,1)S(1)}, bf16[32,1792]{1,0:T(8,128)(2,1)S(1)}, u32[]{:S(2)}, u32[]{:S(2)}) %collective-permute-start.1) | collective-permute-done | bytes 114720 | tf_op jit(solution)/shard_map/ppermute | solution.py:11
  34.8 2.7 %collective-permute-start.2 = (bf16[96,1792]{1,0:T(8,128)(2,1)S(1)}, bf16[96,1792]{1,0:T(8,128)(2,1)S(1)}, u32[]{:S(2)}, u32[]{:S(2)}) collective-permute-start(bf16[96,1792]{1,0:T(8,128)(2,1)S(1)} %pad_maximum_fusion), channel_id=1, source_target_pairs={{0,3},{1,0},{2,1},{3,2},{4,7},{5,4},{6,5},{7,6},{8,11},{9,8},{10,9... | collective-permute-start | bytes 1032200 | tf_op jit(solution)/shard_map/ppermute | solution.py:11
  37.6 3.0 %collective-permute-start.3 = (bf16[96,1792]{1,0:T(8,128)(2,1)S(1)}, bf16[96,1792]{1,0:T(8,128)(2,1)S(1)}, u32[]{:S(2)}, u32[]{:S(2)}) collective-permute-start(bf16[96,1792]{1,0:T(8,128)(2,1)S(1)} %pad_maximum_fusion), channel_id=1, source_target_pairs={{0,2},{1,3},{2,0},{3,1},{4,6},{5,7},{6,4},{7,5},{8,10},{9,11},{10,... | collective-permute-start | bytes 1032200 | tf_op jit(solution)/shard_map/ppermute | solution.py:11
  40.6 4.0 %collective-permute-start.4 = (bf16[96,1792]{1,0:T(8,128)(2,1)S(1)}, bf16[96,1792]{1,0:T(8,128)(2,1)S(1)}, u32[]{:S(2)}, u32[]{:S(2)}) collective-permute-start(bf16[96,1792]{1,0:T(8,128)(2,1)S(1)} %pad_maximum_fusion), channel_id=1, source_target_pairs={{0,1},{1,2},{2,3},{3,0},{4,5},{5,6},{6,7},{7,4},{8,9},{9,10},{10,1... | collective-permute-start | bytes 1032200 | tf_op jit(solution)/shard_map/ppermute | solution.py:11
  44.6 0.7 constant_dynamic-update-slice_fusion.4
  45.3 0.7 constant_dynamic-update-slice_fusion.3
  45.9 7.5 %collective-permute-done.2 = bf16[96,1792]{1,0:T(8,128)(2,1)S(1)} collective-permute-done((bf16[96,1792]{1,0:T(8,128)(2,1)S(1)}, bf16[96,1792]{1,0:T(8,128)(2,1)S(1)}, u32[]{:S(2)}, u32[]{:S(2)}) %collective-permute-start.2) | collective-permute-done | bytes 344096 | tf_op jit(solution)/shard_map/ppermute | solution.py:11
  53.4 0.8 constant_dynamic-update-slice_fusion.2
  54.2 0.0 collective-permute-done.3
  54.2 0.8 constant_dynamic-update-slice_fusion.1
  54.9 0.5 collective-permute-done.4
  55.4 0.8 constant_dynamic-update-slice_fusion
  56.1 0.0 all-to-all-done.1
  56.2 0.1 fusion.2
  56.3 0.2 fusion.1
  56.5 0.9 convolution_convert_fusion.1
  57.4 0.0 copy-start.5
  57.5 1.0 fusion.14
  58.5 4.3 %collective-permute-start.5 = (bf16[96,1792]{1,0:T(8,128)(2,1)}, bf16[96,1792]{1,0:T(8,128)(2,1)S(1)}, u32[]{:S(2)}, u32[]{:S(2)}) collective-permute-start(bf16[96,1792]{1,0:T(8,128)(2,1)} %get-tuple-element.6), channel_id=1, source_target_pairs={{0,1},{1,2},{2,3},{3,0},{4,5},{5,6},{6,7},{7,4},{8,9},{9,10},{10,1... | collective-permute-start | bytes 1032200 | tf_op jit(solution)/shard_map/ppermute | solution.py:11
  62.8 2.1 %collective-permute-start.6 = (bf16[96,1792]{1,0:T(8,128)(2,1)}, bf16[96,1792]{1,0:T(8,128)(2,1)S(1)}, u32[]{:S(2)}, u32[]{:S(2)}) collective-permute-start(bf16[96,1792]{1,0:T(8,128)(2,1)} %get-tuple-element.8), channel_id=1, source_target_pairs={{0,2},{1,3},{2,0},{3,1},{4,6},{5,7},{6,4},{7,5},{8,10},{9,11},{10,... | collective-permute-start | bytes 1032200 | tf_op jit(solution)/shard_map/ppermute | solution.py:11
  64.9 2.6 %collective-permute-start.7 = (bf16[96,1792]{1,0:T(8,128)(2,1)}, bf16[96,1792]{1,0:T(8,128)(2,1)}, u32[]{:S(2)}, u32[]{:S(2)}) collective-permute-start(bf16[96,1792]{1,0:T(8,128)(2,1)} %get-tuple-element.7), channel_id=1, source_target_pairs={{0,3},{1,0},{2,1},{3,2},{4,7},{5,4},{6,5},{7,6},{8,11},{9,8},{10,9... | collective-permute-start | bytes 1032200 | tf_op jit(solution)/shard_map/ppermute | solution.py:11
  67.5 0.9 convolution_convert_fusion.2
  68.4 0.2 fusion.4
  68.5 0.2 fusion.3
  68.7 0.8 copy.21
  69.5 10.9 %all-to-all-start = ((bf16[12,32,512]{2,1,0:T(8,128)(2,1)}), bf16[12,32,512]{2,1,0:T(8,128)(2,1)S(1)}, u32[]{:S(2)}, u32[]{:S(2)}) async-start(bf16[12,32,512]{2,1,0:T(8,128)(2,1)} %bitcast.2), calls=%async_computation | async-start | bytes 786432 | tf_op jit(solution)/shard_map/all_to_all | solution.py:56
  80.4 0.0 collective-permute-done.5
  80.4 0.7 copy-done.4
  81.1 0.9 collective-permute-done.7
  82.0 1.4 %add_convert_fusion = bf16[96,1792]{1,0:T(8,128)(2,1)S(1)} fusion(bf16[96,1792]{1,0:T(8,128)(2,1)} %collective-permute-done.7, bf16[96,1792]{1,0:T(8,128)(2,1)} %copy-done.4, bf16[96,1792]{1,0:T(8,128)(2,1)S(1)} %collective-permute-done.5, bf16[384,1792]{1,0:T(8,128)(2,1)} %copy-done.1), kind=kLoop, calls=%fused_computation.11 | loop fusion | flops 1376256 | bytes 1720320 | tf_op jit(solution)/shard_map/convert_element_type | solution.py:46
  83.4 0.7 fusion.15
  84.0 9.4 %collective-permute-start.8 = (bf16[32,1792]{1,0:T(8,128)(2,1)}, bf16[32,1792]{1,0:T(8,128)(2,1)S(1)}, u32[]{:S(2)}, u32[]{:S(2)}) collective-permute-start(bf16[32,1792]{1,0:T(8,128)(2,1)} %get-tuple-element.11), channel_id=1, source_target_pairs={{0,4},{4,8},{8,0},{1,5},{5,9},{9,1},{2,6},{6,10},{10,2},{3,7},{7,1... | collective-permute-start | bytes 344072 | tf_op jit(solution)/shard_map/ppermute | solution.py:11
  93.5 0.0 copy-start.2
  93.5 0.0 copy-start.3
  93.5 2.3 %collective-permute-start.9 = (bf16[32,1792]{1,0:T(8,128)(2,1)S(1)}, bf16[32,1792]{1,0:T(8,128)(2,1)S(1)}, u32[]{:S(2)}, u32[]{:S(2)}) collective-permute-start(bf16[32,1792]{1,0:T(8,128)(2,1)S(1)} %get-tuple-element.12), channel_id=1, source_target_pairs={{0,8},{4,0},{8,4},{1,9},{5,1},{9,5},{2,10},{6,2},{10,6},{3,11},{7,... | collective-permute-start | bytes 344072 | tf_op jit(solution)/shard_map/ppermute | solution.py:11
  95.8 2.4 %convolution_convert_fusion = bf16[1792,512]{1,0:T(8,128)(2,1)} fusion(bf16[384,1792]{1,0:T(8,128)(2,1)S(1)} %copy-done.6, bf16[384,512]{1,0:T(8,128)(2,1)S(1)} %bitcast.22), kind=kOutput, calls=%fused_computation | convolution fusion | flops 705560576 | bytes 3604480 | tf_op jit(solution)/shard_map/dot_general | solution.py:59
  98.2 0.8 copy.22
  98.9 6.9 %collective-permute-done.8 = bf16[32,1792]{1,0:T(8,128)(2,1)S(1)} collective-permute-done((bf16[32,1792]{1,0:T(8,128)(2,1)}, bf16[32,1792]{1,0:T(8,128)(2,1)S(1)}, u32[]{:S(2)}, u32[]{:S(2)}) %collective-permute-start.8) | collective-permute-done | bytes 114720 | tf_op jit(solution)/shard_map/ppermute | solution.py:11
  105.8 4.1 %collective-permute-done.9 = bf16[32,1792]{1,0:T(8,128)(2,1)S(1)} collective-permute-done((bf16[32,1792]{1,0:T(8,128)(2,1)S(1)}, bf16[32,1792]{1,0:T(8,128)(2,1)S(1)}, u32[]{:S(2)}, u32[]{:S(2)}) %collective-permute-start.9) | collective-permute-done | bytes 114720 | tf_op jit(solution)/shard_map/ppermute | solution.py:11
  109.9 0.8 multiply_convert_fusion
  (13 shorter events, 0.1 us)
Async XLA Ops:
  0.6 55.9 %copy-start = (bf16[1792,512]{1,0:T(8,128)(2,1)S(1)}, bf16[1792,512]{1,0:T(8,128)(2,1)}, u32[]{:S(2)}) copy-start(bf16[1792,512]{1,0:T(8,128)(2,1)} %param.6) | copy-start | bytes 5505028
  2.5 28.9 %collective-permute-start = (bf16[32,1792]{1,0:T(8,128)(2,1)S(1)}, bf16[32,1792]{1,0:T(8,128)(2,1)S(1)}, u32[]{:S(2)}, u32[]{:S(2)}) collective-permute-start(bf16[32,1792]{1,0:T(8,128)(2,1)S(1)} %get-tuple-element.5), channel_id=1, source_target_pairs={{0,8},{4,0},{8,4},{1,9},{5,1},{9,5},{2,10},{6,2},{10,6},{3,11},{7,... | collective-permute-start | bytes 344072 | tf_op jit(solution)/shard_map/ppermute | solution.py:11
  17.0 17.8 %collective-permute-start.1 = (bf16[32,1792]{1,0:T(8,128)(2,1)S(1)}, bf16[32,1792]{1,0:T(8,128)(2,1)S(1)}, u32[]{:S(2)}, u32[]{:S(2)}) collective-permute-start(bf16[32,1792]{1,0:T(8,128)(2,1)S(1)} %get-tuple-element.5), channel_id=1, source_target_pairs={{0,4},{4,8},{8,0},{1,5},{5,9},{9,1},{2,6},{6,10},{10,2},{3,7},{7,1... | collective-permute-start | bytes 344072 | tf_op jit(solution)/shard_map/ppermute | solution.py:11
  21.2 35.0 %all-to-all-start.1 = ((bf16[12,32,512]{2,1,0:T(8,128)(2,1)}), bf16[12,32,512]{2,1,0:T(8,128)(2,1)S(1)}, u32[]{:S(2)}, u32[]{:S(2)}) async-start(bf16[12,32,512]{2,1,0:T(8,128)(2,1)} %copy.16), calls=%async_computation.1 | async-start | bytes 786432 | tf_op jit(solution)/shard_map/all_to_all | solution.py:30
  34.8 18.6 %collective-permute-start.2 = (bf16[96,1792]{1,0:T(8,128)(2,1)S(1)}, bf16[96,1792]{1,0:T(8,128)(2,1)S(1)}, u32[]{:S(2)}, u32[]{:S(2)}) collective-permute-start(bf16[96,1792]{1,0:T(8,128)(2,1)S(1)} %pad_maximum_fusion), channel_id=1, source_target_pairs={{0,3},{1,0},{2,1},{3,2},{4,7},{5,4},{6,5},{7,6},{8,11},{9,8},{10,9... | collective-permute-start | bytes 1032200 | tf_op jit(solution)/shard_map/ppermute | solution.py:11
  37.6 16.6 %collective-permute-start.3 = (bf16[96,1792]{1,0:T(8,128)(2,1)S(1)}, bf16[96,1792]{1,0:T(8,128)(2,1)S(1)}, u32[]{:S(2)}, u32[]{:S(2)}) collective-permute-start(bf16[96,1792]{1,0:T(8,128)(2,1)S(1)} %pad_maximum_fusion), channel_id=1, source_target_pairs={{0,2},{1,3},{2,0},{3,1},{4,6},{5,7},{6,4},{7,5},{8,10},{9,11},{10,... | collective-permute-start | bytes 1032200 | tf_op jit(solution)/shard_map/ppermute | solution.py:11
  40.6 14.8 %collective-permute-start.4 = (bf16[96,1792]{1,0:T(8,128)(2,1)S(1)}, bf16[96,1792]{1,0:T(8,128)(2,1)S(1)}, u32[]{:S(2)}, u32[]{:S(2)}) collective-permute-start(bf16[96,1792]{1,0:T(8,128)(2,1)S(1)} %pad_maximum_fusion), channel_id=1, source_target_pairs={{0,1},{1,2},{2,3},{3,0},{4,5},{5,6},{6,7},{7,4},{8,9},{9,10},{10,1... | collective-permute-start | bytes 1032200 | tf_op jit(solution)/shard_map/ppermute | solution.py:11
  57.4 10.9 %copy-start.1 = (bf16[384,1792]{1,0:T(8,128)(2,1)}, bf16[384,1792]{1,0:T(8,128)(2,1)S(1)}, u32[]{:S(2)}) copy-start(bf16[384,1792]{1,0:T(8,128)(2,1)S(1)} %convolution_convert_fusion.1) | copy-start | bytes 4128772
  57.4 10.0 %copy-start.5 = (bf16[384,1792]{1,0:T(8,128)(2,1)S(1)}, bf16[384,1792]{1,0:T(8,128)(2,1)}, u32[]{:S(2)}) copy-start(bf16[384,1792]{1,0:T(8,128)(2,1)} %constant_dynamic-update-slice_fusion) | copy-start | bytes 4128772
  58.5 21.9 %collective-permute-start.5 = (bf16[96,1792]{1,0:T(8,128)(2,1)}, bf16[96,1792]{1,0:T(8,128)(2,1)S(1)}, u32[]{:S(2)}, u32[]{:S(2)}) collective-permute-start(bf16[96,1792]{1,0:T(8,128)(2,1)} %get-tuple-element.6), channel_id=1, source_target_pairs={{0,1},{1,2},{2,3},{3,0},{4,5},{5,6},{6,7},{7,4},{8,9},{9,10},{10,1... | collective-permute-start | bytes 1032200 | tf_op jit(solution)/shard_map/ppermute | solution.py:11
  62.8 17.6 %collective-permute-start.6 = (bf16[96,1792]{1,0:T(8,128)(2,1)}, bf16[96,1792]{1,0:T(8,128)(2,1)S(1)}, u32[]{:S(2)}, u32[]{:S(2)}) collective-permute-start(bf16[96,1792]{1,0:T(8,128)(2,1)} %get-tuple-element.8), channel_id=1, source_target_pairs={{0,2},{1,3},{2,0},{3,1},{4,6},{5,7},{6,4},{7,5},{8,10},{9,11},{10,... | collective-permute-start | bytes 1032200 | tf_op jit(solution)/shard_map/ppermute | solution.py:11
  64.9 17.1 %collective-permute-start.7 = (bf16[96,1792]{1,0:T(8,128)(2,1)}, bf16[96,1792]{1,0:T(8,128)(2,1)}, u32[]{:S(2)}, u32[]{:S(2)}) collective-permute-start(bf16[96,1792]{1,0:T(8,128)(2,1)} %get-tuple-element.7), channel_id=1, source_target_pairs={{0,3},{1,0},{2,1},{3,2},{4,7},{5,4},{6,5},{7,6},{8,11},{9,8},{10,9... | collective-permute-start | bytes 1032200 | tf_op jit(solution)/shard_map/ppermute | solution.py:11
  69.5 28.7 %all-to-all-start = ((bf16[12,32,512]{2,1,0:T(8,128)(2,1)}), bf16[12,32,512]{2,1,0:T(8,128)(2,1)S(1)}, u32[]{:S(2)}, u32[]{:S(2)}) async-start(bf16[12,32,512]{2,1,0:T(8,128)(2,1)} %bitcast.2), calls=%async_computation | async-start | bytes 786432 | tf_op jit(solution)/shard_map/all_to_all | solution.py:56
  80.4 15.4 %copy-start.6 = (bf16[384,1792]{1,0:T(8,128)(2,1)S(1)}, bf16[384,1792]{1,0:T(8,128)(2,1)}, u32[]{:S(2)}) copy-start(bf16[384,1792]{1,0:T(8,128)(2,1)} %constant_dynamic-update-slice_fusion) | copy-start | bytes 4128772
  80.4 0.7 copy-start.4
  84.0 21.8 %collective-permute-start.8 = (bf16[32,1792]{1,0:T(8,128)(2,1)}, bf16[32,1792]{1,0:T(8,128)(2,1)S(1)}, u32[]{:S(2)}, u32[]{:S(2)}) collective-permute-start(bf16[32,1792]{1,0:T(8,128)(2,1)} %get-tuple-element.11), channel_id=1, source_target_pairs={{0,4},{4,8},{8,0},{1,5},{5,9},{9,1},{2,6},{6,10},{10,2},{3,7},{7,1... | collective-permute-start | bytes 344072 | tf_op jit(solution)/shard_map/ppermute | solution.py:11
  93.5 16.5 %copy-start.2 = (bf16[32,1792]{1,0:T(8,128)(2,1)S(1)}, bf16[32,1792]{1,0:T(8,128)(2,1)}, u32[]{:S(2)}) copy-start(bf16[32,1792]{1,0:T(8,128)(2,1)} %param.5) | copy-start | bytes 344068
  93.5 16.5 %copy-start.3 = (bf16[32,1792]{1,0:T(8,128)(2,1)S(1)}, bf16[32,1792]{1,0:T(8,128)(2,1)}, u32[]{:S(2)}) copy-start(bf16[32,1792]{1,0:T(8,128)(2,1)} %param.4) | copy-start | bytes 344068
  93.5 16.4 %collective-permute-start.9 = (bf16[32,1792]{1,0:T(8,128)(2,1)S(1)}, bf16[32,1792]{1,0:T(8,128)(2,1)S(1)}, u32[]{:S(2)}, u32[]{:S(2)}) collective-permute-start(bf16[32,1792]{1,0:T(8,128)(2,1)S(1)} %get-tuple-element.12), channel_id=1, source_target_pairs={{0,8},{4,0},{8,4},{1,9},{5,1},{9,5},{2,10},{6,2},{10,6},{3,11},{7,... | collective-permute-start | bytes 344072 | tf_op jit(solution)/shard_map/ppermute | solution.py:11

commit v3 on v2

v3 whole, which is shorter than its diff:
```python
import jax
import jax.numpy as jnp
from jax import lax
from jax.experimental import pallas as pl
from jax.experimental.pallas import tpu as pltpu
from jax.sharding import Mesh, PartitionSpec as P

PLANES = 3
BLOCK_COST = 40 << 20
SUM_COST = 100 << 20
GROUP = ("plane", "line")
VMEM = pl.BlockSpec(memory_space=pltpu.VMEM)
SMEM = pl.BlockSpec(memory_space=pltpu.SMEM)
CHUNK = 256


def shift(value, axis, size, step):
    return lax.ppermute(value, axis, [(i, (i + step) % size) for i in range(size)])


def planes(value, step):
    return shift(value, "plane", PLANES, step)


def exchange(value, axis):
    return lax.all_to_all(value, axis, 0, 0, tiled=True)


def together(*values):
    return lax.optimization_barrier(values)


def add_up(terms):
    return sum(t.astype(jnp.float32) for t in terms)


def whole(kernel, place, args, outs, scratch=(), flops=0, moved=1 << 20):
    return pl.pallas_call(
        kernel,
        out_shape=outs,
        in_specs=[SMEM] + [VMEM] * len(args),
        out_specs=jax.tree.map(lambda _: VMEM, outs),
        scratch_shapes=list(scratch),
        compiler_params=pltpu.CompilerParams(vmem_limit_bytes=24 << 20),
        cost_estimate=pl.CostEstimate(flops=flops, bytes_accessed=moved, transcendentals=0),
    )(place, *args)


def block_kernel(place, rows, blocks):
    width = blocks.shape[2]
    for b in range(blocks.shape[0]):
        blocks[b] = rows[:, b * width : (b + 1) * width]


def partial_kernel(place, got, weight, stay, first, second, third, ordered):
    rows = got.shape[1]
    held = PLANES * rows
    line = ordered.shape[0] // held
    for k in range(line):
        for j in range(PLANES):
            at = k * held + j * rows
            source = lax.rem(place[0] + j, PLANES) * line + lax.rem(place[1] + k, line)
            ordered[at : at + rows, :] = got[source]
    for c in range(weight.shape[0] // CHUNK):
        span = slice(c * CHUNK, (c + 1) * CHUNK)
        part = lax.dot_general(
            ordered[...],
            weight[span, :],
            (((1,), (1,)), ((), ())),
            preferred_element_type=jnp.float32,
        ).astype(jnp.bfloat16)
        for k, piece in enumerate((stay, first, second, third)):
            piece[:, span] = part[k * held : (k + 1) * held]


def column_kernel(place, own, first, second, third, weight, columns, every):
    rows = columns.shape[1]
    held = PLANES * rows
    line = every.shape[0] // held
    for k, piece in enumerate((own, first, second, third)):
        every[k * held : (k + 1) * held, :] = piece[...]
    for c in range(weight.shape[1] // CHUNK):
        span = slice(c * CHUNK, (c + 1) * CHUNK)
        part = jnp.dot(
            every[...], weight[:, span], preferred_element_type=jnp.float32
        ).astype(jnp.bfloat16)
        for k in range(line):
            for j in range(PLANES):
                at = k * held + j * rows
                owner = lax.rem(place[0] + j, PLANES) * line + lax.rem(place[1] + k, line)
                columns[owner, :, span] = part[at : at + rows]


def output_kernel(place, columns, output):
    width = columns.shape[2]
    for b in range(columns.shape[0]):
        output[:, b * width : (b + 1) * width] = columns[b]


def body(gate_pre, up_pre, down_weight, out_grad):
    rows, hidden_width = gate_pre.shape
    width = down_weight.shape[1]
    group = out_grad.shape[1] // width
    line = group // PLANES
    place = jnp.stack([lax.axis_index("plane"), lax.axis_index("line")]).astype(jnp.int32)

    def made(*shape):
        return jax.ShapeDtypeStruct(shape, jnp.bfloat16)

    gate_vals = gate_pre.astype(jnp.float32)
    up_vals = up_pre.astype(jnp.float32)
    sig = jax.nn.sigmoid(gate_vals)
    act = gate_vals * sig
    hidden = (act * up_vals).astype(jnp.bfloat16)

    hidden, out_grad = together(hidden, out_grad)
    by_plane = [hidden] + [planes(hidden, -j) for j in range(1, PLANES)]

    blocks = whole(block_kernel, place, [out_grad], made(group, rows, width), moved=BLOCK_COST)
    by_plane[1], by_plane[2], blocks = together(by_plane[1], by_plane[2], blocks)
    got = exchange(blocks, GROUP)

    mine = jnp.concatenate(by_plane, axis=0)
    by_line = [shift(mine, "line", line, -k) for k in range(1, line)]

    *sums, cotangent = whole(
        partial_kernel,
        place,
        [got, down_weight],
        [made(PLANES * rows, hidden_width)] * line + [made(group * rows, width)],
        flops=2 * group * rows * width * hidden_width,
        moved=SUM_COST,
    )
    line_sums = [sums[0]] + [shift(sums[k], "line", line, k) for k in range(1, line)]
    line_sum = [
        add_up([s[j * rows : (j + 1) * rows] for s in line_sums]).astype(jnp.bfloat16)
        for j in range(PLANES)
    ]
    hidden_grad = add_up(together(line_sum[0], planes(line_sum[1], 1), planes(line_sum[2], 2)))

    by_line = together(*by_line, sums[0])[:-1]
    columns, hidden_all = whole(
        column_kernel,
        place,
        [mine, *by_line, down_weight],
        [made(group, rows, width), made(group * rows, hidden_width)],
        flops=2 * group * rows * width * hidden_width,
        moved=4 << 20,
    )
    columns = exchange(columns, GROUP)
    weight_grad = lax.dot_general(
        hidden_all, cotangent, (((0,), (0,)), ((), ())), preferred_element_type=jnp.float32
    ).astype(jnp.bfloat16)
    output = whole(output_kernel, place, [columns], made(rows, group * width))

    gate_grad = (hidden_grad * up_vals * sig * (1.0 + gate_vals * (1.0 - sig))).astype(jnp.bfloat16)
    up_grad = (hidden_grad * act).astype(jnp.bfloat16)
    return (output, gate_grad, up_grad, weight_grad)


BLOCK_COST = 1 << 20


def solution(mesh):
    tokens = ("dp",) + GROUP
    fine = Mesh(mesh.devices.reshape(mesh.shape["dp"], PLANES, -1), tokens)
    return jax.shard_map(
        body,
        mesh=fine,
        in_specs=(P(tokens, None), P(tokens, None), P(None, GROUP), P(tokens, None)),
        out_specs=(P(tokens, None), P(tokens, None), P(tokens, None), P(None, tokens)),
        check_vma=False,
    )
```

time: 111 us -> 108 us (0.973)
  Pallas kernels: 0 us -> 7.7 us
  local copies, waits for them, and re-layouts: 9.81 us -> 2.86 us
  starting transfers between devices: 68 us -> 64.7 us
  waiting for transfers between devices: 23.3 us -> 25.4 us
  matrix products: 4.15 us -> 2.37 us
  other arithmetic: 4.65 us -> 3.54 us
    pallas_call x0 -> x4, Pallas kernels: none -> 7.7 us  [whole(): pl.pallas_call(kernel, out_shape=outs, in_specs=[SMEM] + [VMEM] * len(arg...]
    all_to_all x2, waiting for transfers between devices: 0.01 us -> 6.37 us  [exchange(): return lax.all_to_all(value, axis, 0, 0, tiled=True)]
    ppermute x10, waiting for transfers between devices: 23.3 us -> 19 us  [shift(): lax.ppermute(value, axis, [(i, (i + step) % size) for i in range(size)])]
    ppermute x10, starting transfers between devices: 46.9 us -> 43.9 us  [shift(): lax.ppermute(value, axis, [(i, (i + step) % size) for i in range(size)])]
    reshape x2 -> x0, local copies, waits for them, and re-layouts: 2.05 us -> none  [the longest x1 1.27 us: body(): blocks = jnp.swapaxes(out_grad.reshape(rows, group, width), 0, 1)]
    unnamed x1 -> x0, other arithmetic: 1.81 us -> none
    dot_general x2 -> x0, matrix products: 1.78 us -> none  [the longest x1 0.91 us: body(): lax.dot_general(cotangent, down_weight, (((1,), (1,)), ((), ())), preferr...]
    slice x2 -> x0, local copies, waits for them, and re-layouts: 1.67 us -> none  [the longest x1 1 us: body(): partial_sums[k]]
  transfers between devices with their start and end apart: 12 -> 12, of which waited for: 6 -> 4; matrix products, arithmetic and copies ran while one was open for 12% -> 4% of each run, Pallas kernels for 0% -> 6%
where the time goes in v3:
time: 108 us; the launch traced here: 107 us
  starting transfers between devices  64.7 us (60%)
  waiting for transfers between devices  25.4 us (24%)
  Pallas kernels  7.7 us (7%)
  other arithmetic  3.54 us (3%)
  local copies, waits for them, and re-layouts  2.86 us (3%)
  matrix products  2.37 us (2%)
    ppermute x10, starting transfers between devices, shift(): lax.ppermute(value, axis, [(i, (i + step) % size) for i in range(size)])  43.9 us
    all_to_all x2, starting transfers between devices, exchange(): return lax.all_to_all(value, axis, 0, 0, tiled=True)  20.8 us
    ppermute x10, waiting for transfers between devices, shift(): lax.ppermute(value, axis, [(i, (i + step) % size) for i in range(size)])  19 us
    pallas_call x4, Pallas kernels, whole(): pl.pallas_call(kernel, out_shape=outs, in_specs=[SMEM] + [VMEM] * len(arg...  7.7 us
    all_to_all x2, waiting for transfers between devices, exchange(): return lax.all_to_all(value, axis, 0, 0, tiled=True)  6.37 us
    unnamed x18, local copies, waits for them, and re-layouts  2.85 us
    dot_general x1, matrix products, body(): lax.dot_general(hidden_all, cotangent, (((0,), (0,)), ((), ())), preferre...  2.37 us
  transfers between devices with their start and end apart: 12, of which 4 were waited for; matrix products, arithmetic and copies ran while one was open for 4% of the time, Pallas kernels for 6%

profile of v3, /device:TPU:6, one launch (start us, length us, event | category | flops | bytes accessed | tf_op | source)
XLA Modules:
  0.0 107.4 jit_solution(2495697490604116027)
XLA Ops:
  0.6 0.0 copy-start
  0.6 1.2 %fusion = bf16[32,1792]{1,0:T(8,128)(2,1)S(1)} fusion(bf16[32,1792]{1,0:T(8,128)(2,1)} %param.5, bf16[32,1792]{1,0:T(8,128)(2,1)} %param.4), kind=kLoop, calls=%fused_computation.6 | loop fusion | flops 458752 | bytes 344064 | tf_op jit(solution)/shard_map/convert_element_type | solution.py:114
  1.8 10.9 %collective-permute-start.1 = (bf16[32,1792]{1,0:T(8,128)(2,1)S(1)}, bf16[32,1792]{1,0:T(8,128)(2,1)S(1)}, u32[]{:S(2)}, u32[]{:S(2)}) collective-permute-start(bf16[32,1792]{1,0:T(8,128)(2,1)S(1)} %fusion), channel_id=1, source_target_pairs={{0,4},{4,8},{8,0},{1,5},{5,9},{9,1},{2,6},{6,10},{10,2},{3,7},{7,1... | collective-permute-start | bytes 344072 | tf_op jit(solution)/shard_map/ppermute | solution.py:18
  12.7 5.6 %collective-permute-start = (bf16[32,1792]{1,0:T(8,128)(2,1)S(1)}, bf16[32,1792]{1,0:T(8,128)(2,1)S(1)}, u32[]{:S(2)}, u32[]{:S(2)}) collective-permute-start(bf16[32,1792]{1,0:T(8,128)(2,1)S(1)} %fusion), channel_id=1, source_target_pairs={{0,8},{4,0},{8,4},{1,9},{5,1},{9,5},{2,10},{6,2},{10,6},{3,11},{7,... | collective-permute-start | bytes 344072 | tf_op jit(solution)/shard_map/ppermute | solution.py:18
  18.3 0.1 pad_add_fusion.place
  18.4 0.0 copy-start.1
  18.4 1.0 copy-done.1
  19.4 1.3 %shard_map.75 = bf16[12,32,512]{2,1,0:T(8,128)(2,1)} custom-call(s32[2]{0:T(128)S(1)} %pad_add_fusion.place, bf16[32,6144]{1,0:T(8,128)(2,1)S(1)} %copy-done.1), custom_call_target="tpu_custom_call" | custom-call | bytes 1048576 | tf_op jit(solution)/shard_map/pallas_call | solution.py:38
  20.7 0.0 collective-permute-done.1
  20.7 9.3 %collective-permute-done = bf16[32,1792]{1,0:T(8,128)(2,1)S(1)} collective-permute-done((bf16[32,1792]{1,0:T(8,128)(2,1)S(1)}, bf16[32,1792]{1,0:T(8,128)(2,1)S(1)}, u32[]{:S(2)}, u32[]{:S(2)}) %collective-permute-start) | collective-permute-done | bytes 114720 | tf_op jit(solution)/shard_map/ppermute | solution.py:18
  30.0 11.4 %all-to-all-start = ((bf16[12,32,512]{2,1,0:T(8,128)(2,1)}), bf16[12,32,512]{2,1,0:T(8,128)(2,1)S(1)}, u32[]{:S(2)}, u32[]{:S(2)}) async-start(bf16[12,32,512]{2,1,0:T(8,128)(2,1)} %shard_map.75), calls=%async_computation | async-start | bytes 786432 | tf_op jit(solution)/shard_map/all_to_all | solution.py:26
  41.4 2.0 %collective-permute-start.4 = (bf16[96,1792]{1,0:T(8,128)(2,1)S(1)}, bf16[96,1792]{1,0:T(8,128)(2,1)S(1)}, u32[]{:S(2)}, u32[]{:S(2)}) collective-permute-start(bf16[96,1792]{1,0:T(8,128)(2,1)S(1)} %constant_dynamic-update-slice_fusion.own), channel_id=1, source_target_pairs={{0,1},{1,2},{2,3},{3,0},{4,5},{5,6},{6,7},{7,4},{8,9},{9,10},{10,1... | collective-permute-start | bytes 1032200 | tf_op jit(solution)/shard_map/ppermute | solution.py:18
  43.4 4.8 %collective-permute-start.3 = (bf16[96,1792]{1,0:T(8,128)(2,1)S(1)}, bf16[96,1792]{1,0:T(8,128)(2,1)}, u32[]{:S(2)}, u32[]{:S(2)}) collective-permute-start(bf16[96,1792]{1,0:T(8,128)(2,1)S(1)} %constant_dynamic-update-slice_fusion.own), channel_id=1, source_target_pairs={{0,2},{1,3},{2,0},{3,1},{4,6},{5,7},{6,4},{7,5},{8,10},{9,11},{10,... | collective-permute-start | bytes 1032200 | tf_op jit(solution)/shard_map/ppermute | solution.py:18
  48.2 1.9 %collective-permute-start.2 = (bf16[96,1792]{1,0:T(8,128)(2,1)S(1)}, bf16[96,1792]{1,0:T(8,128)(2,1)}, u32[]{:S(2)}, u32[]{:S(2)}) collective-permute-start(bf16[96,1792]{1,0:T(8,128)(2,1)S(1)} %constant_dynamic-update-slice_fusion.own), channel_id=1, source_target_pairs={{0,3},{1,0},{2,1},{3,2},{4,7},{5,4},{6,5},{7,6},{8,11},{9,8},{10,9... | collective-permute-start | bytes 1032200 | tf_op jit(solution)/shard_map/ppermute | solution.py:18
  50.1 6.4 %all-to-all-done.got = bf16[12,32,512]{2,1,0:T(8,128)(2,1)S(1)} async-done(((bf16[12,32,512]{2,1,0:T(8,128)(2,1)}), bf16[12,32,512]{2,1,0:T(8,128)(2,1)S(1)}, u32[]{:S(2)}, u32[]{:S(2)}) %all-to-all-start) | async-done | bytes 393248 | tf_op jit(solution)/shard_map/all_to_all | solution.py:26
  56.5 0.0 copy-done
  56.5 2.3 %shard_map.76 = (bf16[96,1792]{1,0:T(8,128)(2,1)S(1)}, bf16[96,1792]{1,0:T(8,128)(2,1)}, bf16[96,1792]{1,0:T(8,128)(2,1)}, bf16[96,1792]{1,0:T(8,128)(2,1)}, bf16[384,512]{1,0:T(8,128)(2,1)S(1)}) custom-call(s32[2]{0:T(128)S(1)} %pad_add_fusion.place, bf16[12,32,512]{2,1,0:T(8,128)(2,1)S(1)} %all-to-all-done.got, bf16[1792,512]{1,0:T(8,128)(2,1)S(1)} %copy-done), custom_call_target="tpu_custom_call" | custom-call | flops 704643072 | bytes 104857600 | tf_op jit(solution)/shard_map/pallas_call | solution.py:38
  58.8 0.0 copy-start.4
  58.8 0.7 copy-done.4
  59.6 3.8 %collective-permute-start.5 = (bf16[96,1792]{1,0:T(8,128)(2,1)}, bf16[96,1792]{1,0:T(8,128)(2,1)}, u32[]{:S(2)}, u32[]{:S(2)}) collective-permute-start(bf16[96,1792]{1,0:T(8,128)(2,1)} %get-tuple-element.32), channel_id=1, source_target_pairs={{0,1},{1,2},{2,3},{3,0},{4,5},{5,6},{6,7},{7,4},{8,9},{9,10},{10,1... | collective-permute-start | bytes 1032200 | tf_op jit(solution)/shard_map/ppermute | solution.py:18
  63.4 1.9 %collective-permute-start.6 = (bf16[96,1792]{1,0:T(8,128)(2,1)}, bf16[96,1792]{1,0:T(8,128)(2,1)}, u32[]{:S(2)}, u32[]{:S(2)}) collective-permute-start(bf16[96,1792]{1,0:T(8,128)(2,1)} %get-tuple-element.33), channel_id=1, source_target_pairs={{0,2},{1,3},{2,0},{3,1},{4,6},{5,7},{6,4},{7,5},{8,10},{9,11},{10,... | collective-permute-start | bytes 1032200 | tf_op jit(solution)/shard_map/ppermute | solution.py:18
  65.3 0.0 collective-permute-done.4.third
  65.3 3.3 %collective-permute-start.7 = (bf16[96,1792]{1,0:T(8,128)(2,1)}, bf16[96,1792]{1,0:T(8,128)(2,1)}, u32[]{:S(2)}, u32[]{:S(2)}) collective-permute-start(bf16[96,1792]{1,0:T(8,128)(2,1)} %get-tuple-element.34), channel_id=1, source_target_pairs={{0,3},{1,0},{2,1},{3,2},{4,7},{5,4},{6,5},{7,6},{8,11},{9,8},{10,9... | collective-permute-start | bytes 1032200 | tf_op jit(solution)/shard_map/ppermute | solution.py:18
  68.7 0.0 collective-permute-done.3.second
  68.7 0.0 collective-permute-done.2.first
  68.7 2.7 %shard_map.77 = (bf16[12,32,512]{2,1,0:T(8,128)(2,1)}, bf16[384,1792]{1,0:T(8,128)(2,1)S(1)}) custom-call(s32[2]{0:T(128)S(1)} %pad_add_fusion.place, bf16[96,1792]{1,0:T(8,128)(2,1)S(1)} %constant_dynamic-update-slice_fusion.own, bf16[96,1792]{1,0:T(8,128)(2,1)} %collective-permute-done.2.first, bf16[96,1792]{1,0:T(8,128)(2,1)} %collective-permute-done.3.second, ...), custom_call_target="tpu_custom_call" | custom-call | flops 704643072 | bytes 4194304 | tf_op jit(solution)/shard_map/pallas_call | solution.py:38
  71.4 0.0 copy-start.2
  71.4 1.1 %copy-done.2 = bf16[384,1792]{1,0:T(8,128)(2,1)} copy-done((bf16[384,1792]{1,0:T(8,128)(2,1)}, bf16[384,1792]{1,0:T(8,128)(2,1)S(1)}, u32[]{:S(2)}) %copy-start.2) | copy-done | bytes 1376280
  72.5 0.0 copy-start.5
  72.5 9.4 %all-to-all-start.1 = ((bf16[12,32,512]{2,1,0:T(8,128)(2,1)}), bf16[12,32,512]{2,1,0:T(8,128)(2,1)S(1)}, u32[]{:S(2)}, u32[]{:S(2)}) async-start(bf16[12,32,512]{2,1,0:T(8,128)(2,1)} %get-tuple-element.31), calls=%async_computation.1 | async-start | bytes 786432 | tf_op jit(solution)/shard_map/all_to_all | solution.py:26
  81.9 0.0 collective-permute-done.5
  81.9 0.0 collective-permute-done.6
  81.9 0.0 collective-permute-done.7
  81.9 1.5 %add_convert_fusion = (bf16[32,1792]{1,0:T(8,128)(2,1)S(1)}, bf16[32,1792]{1,0:T(8,128)(2,1)S(1)}, bf16[32,1792]{1,0:T(8,128)(2,1)S(1)}) fusion(bf16[96,1792]{1,0:T(8,128)(2,1)} %collective-permute-done.7, bf16[96,1792]{1,0:T(8,128)(2,1)} %collective-permute-done.6, bf16[96,1792]{1,0:T(8,128)(2,1)} %collective-permute-done.5, ...), kind=kLoop, calls=%fused_computation.16 | loop fusion | flops 1376256 | bytes 1720320 | tf_op jit(solution)/shard_map/convert_element_type | solution.py:136
  83.4 7.3 %collective-permute-start.9 = (bf16[32,1792]{1,0:T(8,128)(2,1)S(1)}, bf16[32,1792]{1,0:T(8,128)(2,1)S(1)}, u32[]{:S(2)}, u32[]{:S(2)}) collective-permute-start(bf16[32,1792]{1,0:T(8,128)(2,1)S(1)} %get-tuple-element.40), channel_id=1, source_target_pairs={{0,8},{4,0},{8,4},{1,9},{5,1},{9,5},{2,10},{6,2},{10,6},{3,11},{7,... | collective-permute-start | bytes 344072 | tf_op jit(solution)/shard_map/ppermute | solution.py:18
  90.7 2.5 %collective-permute-start.8 = (bf16[32,1792]{1,0:T(8,128)(2,1)S(1)}, bf16[32,1792]{1,0:T(8,128)(2,1)S(1)}, u32[]{:S(2)}, u32[]{:S(2)}) collective-permute-start(bf16[32,1792]{1,0:T(8,128)(2,1)S(1)} %get-tuple-element.41), channel_id=1, source_target_pairs={{0,4},{4,8},{8,0},{1,5},{5,9},{9,1},{2,6},{6,10},{10,2},{3,7},{7,1... | collective-permute-start | bytes 344072 | tf_op jit(solution)/shard_map/ppermute | solution.py:18
  93.1 0.0 copy-done.5
  93.2 0.0 copy-done.3
  93.2 0.0 copy-start.6
  93.2 0.0 copy-start.7
  93.2 2.4 %convolution_convert_fusion = bf16[1792,512]{1,0:T(8,128)(2,1)} fusion(bf16[384,1792]{1,0:T(8,128)(2,1)S(1)} %copy-done.3, bf16[384,512]{1,0:T(8,128)(2,1)S(1)} %copy-done.5), kind=kOutput, calls=%fused_computation | convolution fusion | flops 705560576 | bytes 3604480 | tf_op jit(solution)/shard_map/dot_general | solution.py:151
  95.6 3.2 %collective-permute-done.9 = bf16[32,1792]{1,0:T(8,128)(2,1)S(1)} collective-permute-done((bf16[32,1792]{1,0:T(8,128)(2,1)S(1)}, bf16[32,1792]{1,0:T(8,128)(2,1)S(1)}, u32[]{:S(2)}, u32[]{:S(2)}) %collective-permute-start.9) | collective-permute-done | bytes 114720 | tf_op jit(solution)/shard_map/ppermute | solution.py:18
  98.8 6.5 %collective-permute-done.8 = bf16[32,1792]{1,0:T(8,128)(2,1)S(1)} collective-permute-done((bf16[32,1792]{1,0:T(8,128)(2,1)S(1)}, bf16[32,1792]{1,0:T(8,128)(2,1)S(1)}, u32[]{:S(2)}, u32[]{:S(2)}) %collective-permute-start.8) | collective-permute-done | bytes 114720 | tf_op jit(solution)/shard_map/ppermute | solution.py:18
  105.3 0.0 copy-done.6
  105.3 0.0 copy-done.7
  105.3 0.8 multiply_convert_fusion
  106.1 0.0 all-to-all-done.1.columns
  106.1 1.3 %shard_map.78 = bf16[32,6144]{1,0:T(8,128)(2,1)} custom-call(s32[2]{0:T(128)S(1)} %pad_add_fusion.place, bf16[12,32,512]{2,1,0:T(8,128)(2,1)S(1)} %all-to-all-done.1.columns), custom_call_target="tpu_custom_call" | custom-call | bytes 1048576 | tf_op jit(solution)/shard_map/pallas_call | solution.py:38
  (4 shorter events, 0.0 us)
Async XLA Ops:
  0.6 55.9 %copy-start = (bf16[1792,512]{1,0:T(8,128)(2,1)S(1)}, bf16[1792,512]{1,0:T(8,128)(2,1)}, u32[]{:S(2)}) copy-start(bf16[1792,512]{1,0:T(8,128)(2,1)} %weight.3) | copy-start | bytes 5505028
  1.8 18.9 %collective-permute-start.1 = (bf16[32,1792]{1,0:T(8,128)(2,1)S(1)}, bf16[32,1792]{1,0:T(8,128)(2,1)S(1)}, u32[]{:S(2)}, u32[]{:S(2)}) collective-permute-start(bf16[32,1792]{1,0:T(8,128)(2,1)S(1)} %fusion), channel_id=1, source_target_pairs={{0,4},{4,8},{8,0},{1,5},{5,9},{9,1},{2,6},{6,10},{10,2},{3,7},{7,1... | collective-permute-start | bytes 344072 | tf_op jit(solution)/shard_map/ppermute | solution.py:18
  12.7 17.3 %collective-permute-start = (bf16[32,1792]{1,0:T(8,128)(2,1)S(1)}, bf16[32,1792]{1,0:T(8,128)(2,1)S(1)}, u32[]{:S(2)}, u32[]{:S(2)}) collective-permute-start(bf16[32,1792]{1,0:T(8,128)(2,1)S(1)} %fusion), channel_id=1, source_target_pairs={{0,8},{4,0},{8,4},{1,9},{5,1},{9,5},{2,10},{6,2},{10,6},{3,11},{7,... | collective-permute-start | bytes 344072 | tf_op jit(solution)/shard_map/ppermute | solution.py:18
  18.4 1.0 copy-start.1
  30.0 26.5 %all-to-all-start = ((bf16[12,32,512]{2,1,0:T(8,128)(2,1)}), bf16[12,32,512]{2,1,0:T(8,128)(2,1)S(1)}, u32[]{:S(2)}, u32[]{:S(2)}) async-start(bf16[12,32,512]{2,1,0:T(8,128)(2,1)} %shard_map.75), calls=%async_computation | async-start | bytes 786432 | tf_op jit(solution)/shard_map/all_to_all | solution.py:26
  41.4 23.9 %collective-permute-start.4 = (bf16[96,1792]{1,0:T(8,128)(2,1)S(1)}, bf16[96,1792]{1,0:T(8,128)(2,1)S(1)}, u32[]{:S(2)}, u32[]{:S(2)}) collective-permute-start(bf16[96,1792]{1,0:T(8,128)(2,1)S(1)} %constant_dynamic-update-slice_fusion.own), channel_id=1, source_target_pairs={{0,1},{1,2},{2,3},{3,0},{4,5},{5,6},{6,7},{7,4},{8,9},{9,10},{10,1... | collective-permute-start | bytes 1032200 | tf_op jit(solution)/shard_map/ppermute | solution.py:18
  43.4 25.3 %collective-permute-start.3 = (bf16[96,1792]{1,0:T(8,128)(2,1)S(1)}, bf16[96,1792]{1,0:T(8,128)(2,1)}, u32[]{:S(2)}, u32[]{:S(2)}) collective-permute-start(bf16[96,1792]{1,0:T(8,128)(2,1)S(1)} %constant_dynamic-update-slice_fusion.own), channel_id=1, source_target_pairs={{0,2},{1,3},{2,0},{3,1},{4,6},{5,7},{6,4},{7,5},{8,10},{9,11},{10,... | collective-permute-start | bytes 1032200 | tf_op jit(solution)/shard_map/ppermute | solution.py:18
  48.2 20.5 %collective-permute-start.2 = (bf16[96,1792]{1,0:T(8,128)(2,1)S(1)}, bf16[96,1792]{1,0:T(8,128)(2,1)}, u32[]{:S(2)}, u32[]{:S(2)}) collective-permute-start(bf16[96,1792]{1,0:T(8,128)(2,1)S(1)} %constant_dynamic-update-slice_fusion.own), channel_id=1, source_target_pairs={{0,3},{1,0},{2,1},{3,2},{4,7},{5,4},{6,5},{7,6},{8,11},{9,8},{10,9... | collective-permute-start | bytes 1032200 | tf_op jit(solution)/shard_map/ppermute | solution.py:18
  58.8 0.7 copy-start.4
  59.6 22.3 %collective-permute-start.5 = (bf16[96,1792]{1,0:T(8,128)(2,1)}, bf16[96,1792]{1,0:T(8,128)(2,1)}, u32[]{:S(2)}, u32[]{:S(2)}) collective-permute-start(bf16[96,1792]{1,0:T(8,128)(2,1)} %get-tuple-element.32), channel_id=1, source_target_pairs={{0,1},{1,2},{2,3},{3,0},{4,5},{5,6},{6,7},{7,4},{8,9},{9,10},{10,1... | collective-permute-start | bytes 1032200 | tf_op jit(solution)/shard_map/ppermute | solution.py:18
  63.4 18.5 %collective-permute-start.6 = (bf16[96,1792]{1,0:T(8,128)(2,1)}, bf16[96,1792]{1,0:T(8,128)(2,1)}, u32[]{:S(2)}, u32[]{:S(2)}) collective-permute-start(bf16[96,1792]{1,0:T(8,128)(2,1)} %get-tuple-element.33), channel_id=1, source_target_pairs={{0,2},{1,3},{2,0},{3,1},{4,6},{5,7},{6,4},{7,5},{8,10},{9,11},{10,... | collective-permute-start | bytes 1032200 | tf_op jit(solution)/shard_map/ppermute | solution.py:18
  65.3 16.6 %collective-permute-start.7 = (bf16[96,1792]{1,0:T(8,128)(2,1)}, bf16[96,1792]{1,0:T(8,128)(2,1)}, u32[]{:S(2)}, u32[]{:S(2)}) collective-permute-start(bf16[96,1792]{1,0:T(8,128)(2,1)} %get-tuple-element.34), channel_id=1, source_target_pairs={{0,3},{1,0},{2,1},{3,2},{4,7},{5,4},{6,5},{7,6},{8,11},{9,8},{10,9... | collective-permute-start | bytes 1032200 | tf_op jit(solution)/shard_map/ppermute | solution.py:18
  71.4 1.1 %copy-start.2 = (bf16[384,1792]{1,0:T(8,128)(2,1)}, bf16[384,1792]{1,0:T(8,128)(2,1)S(1)}, u32[]{:S(2)}) copy-start(bf16[384,1792]{1,0:T(8,128)(2,1)S(1)} %get-tuple-element.38) | copy-start | bytes 4128772
  72.5 20.6 %copy-start.5 = (bf16[384,512]{1,0:T(8,128)(2,1)S(1)}, bf16[384,512]{1,0:T(8,128)(2,1)}, u32[]{:S(2)}) copy-start(bf16[384,512]{1,0:T(8,128)(2,1)} %copy-done.4) | copy-start | bytes 1179652
  72.5 20.7 %copy-start.3 = (bf16[384,1792]{1,0:T(8,128)(2,1)S(1)}, bf16[384,1792]{1,0:T(8,128)(2,1)}, u32[]{:S(2)}) copy-start(bf16[384,1792]{1,0:T(8,128)(2,1)} %copy-done.2) | copy-start | bytes 4128772
  72.5 33.6 %all-to-all-start.1 = ((bf16[12,32,512]{2,1,0:T(8,128)(2,1)}), bf16[12,32,512]{2,1,0:T(8,128)(2,1)S(1)}, u32[]{:S(2)}, u32[]{:S(2)}) async-start(bf16[12,32,512]{2,1,0:T(8,128)(2,1)} %get-tuple-element.31), calls=%async_computation.1 | async-start | bytes 786432 | tf_op jit(solution)/shard_map/all_to_all | solution.py:26
  83.4 15.4 %collective-permute-start.9 = (bf16[32,1792]{1,0:T(8,128)(2,1)S(1)}, bf16[32,1792]{1,0:T(8,128)(2,1)S(1)}, u32[]{:S(2)}, u32[]{:S(2)}) collective-permute-start(bf16[32,1792]{1,0:T(8,128)(2,1)S(1)} %get-tuple-element.40), channel_id=1, source_target_pairs={{0,8},{4,0},{8,4},{1,9},{5,1},{9,5},{2,10},{6,2},{10,6},{3,11},{7,... | collective-permute-start | bytes 344072 | tf_op jit(solution)/shard_map/ppermute | solution.py:18
  90.7 14.6 %collective-permute-start.8 = (bf16[32,1792]{1,0:T(8,128)(2,1)S(1)}, bf16[32,1792]{1,0:T(8,128)(2,1)S(1)}, u32[]{:S(2)}, u32[]{:S(2)}) collective-permute-start(bf16[32,1792]{1,0:T(8,128)(2,1)S(1)} %get-tuple-element.41), channel_id=1, source_target_pairs={{0,4},{4,8},{8,0},{1,5},{5,9},{9,1},{2,6},{6,10},{10,2},{3,7},{7,1... | collective-permute-start | bytes 344072 | tf_op jit(solution)/shard_map/ppermute | solution.py:18
  93.2 12.1 %copy-start.6 = (bf16[32,1792]{1,0:T(8,128)(2,1)S(1)}, bf16[32,1792]{1,0:T(8,128)(2,1)}, u32[]{:S(2)}) copy-start(bf16[32,1792]{1,0:T(8,128)(2,1)} %param.5) | copy-start | bytes 344068
  93.2 12.1 %copy-start.7 = (bf16[32,1792]{1,0:T(8,128)(2,1)S(1)}, bf16[32,1792]{1,0:T(8,128)(2,1)}, u32[]{:S(2)}) copy-start(bf16[32,1792]{1,0:T(8,128)(2,1)} %param.4) | copy-start | bytes 344068

commit v4 on v3

--- a/solution.py
+++ b/solution.py
@@ -73,10 +73,9 @@
             piece[:, span] = part[k * held : (k + 1) * held]
 
 
-def column_kernel(place, own, first, second, third, weight, columns, every):
-    rows = columns.shape[1]
+def column_kernel(place, own, first, second, third, weight, stay, up_one, up_two, every):
+    line, rows = stay.shape[0], stay.shape[1]
     held = PLANES * rows
-    line = every.shape[0] // held
     for k, piece in enumerate((own, first, second, third)):
         every[k * held : (k + 1) * held, :] = piece[...]
     for c in range(weight.shape[1] // CHUNK):
@@ -85,16 +84,19 @@
             every[...], weight[:, span], preferred_element_type=jnp.float32
         ).astype(jnp.bfloat16)
         for k in range(line):
-            for j in range(PLANES):
+            x = lax.rem(place[1] + k, line)
+            for j, dest in enumerate((stay, up_two, up_one)):
                 at = k * held + j * rows
-                owner = lax.rem(place[0] + j, PLANES) * line + lax.rem(place[1] + k, line)
-                columns[owner, :, span] = part[at : at + rows]
+                dest[x, :, span] = part[at : at + rows]
 
 
 def output_kernel(place, columns, output):
-    width = columns.shape[2]
-    for b in range(columns.shape[0]):
-        output[:, b * width : (b + 1) * width] = columns[b]
+    line, width = columns.shape[0], columns.shape[3]
+    for plane in range(PLANES):
+        slot = lax.rem(plane - place[0] + PLANES, PLANES)
+        for x in range(line):
+            b = plane * line + x
+            output[:, b * width : (b + 1) * width] = columns[x, slot]
 
 
 def body(gate_pre, up_pre, down_weight, out_grad):
@@ -136,18 +138,20 @@
         add_up([s[j * rows : (j + 1) * rows] for s in line_sums]).astype(jnp.bfloat16)
         for j in range(PLANES)
     ]
-    hidden_grad = add_up(together(line_sum[0], planes(line_sum[1], 1), planes(line_sum[2], 2)))
 
     by_line = together(*by_line, sums[0])[:-1]
-    columns, hidden_all = whole(
+    stay, up_one, up_two, hidden_all = whole(
         column_kernel,
         place,
         [mine, *by_line, down_weight],
-        [made(group, rows, width), made(group * rows, hidden_width)],
+        [made(line, rows, width)] * 3 + [made(group * rows, hidden_width)],
         flops=2 * group * rows * width * hidden_width,
         moved=4 << 20,
     )
-    columns = exchange(columns, GROUP)
+    from_one, from_two = planes(up_one, -1), planes(up_two, -2)
+    *line_sum, stay, hidden_all = together(*line_sum, stay, hidden_all)
+    hidden_grad = add_up(together(line_sum[0], planes(line_sum[1], 1), planes(line_sum[2], 2)))
+    columns = exchange(jnp.stack([stay, from_one, from_two], axis=1), "line")
     weight_grad = lax.dot_general(
         hidden_all, cotangent, (((0,), (0,)), ((), ())), preferred_element_type=jnp.float32
     ).astype(jnp.bfloat16)

time: 108 us -> 107 us (level)
  the two profiles are of different devices: /device:TPU:6 before, /device:TPU:136 now
where the time goes in v4:
time: 107 us; the launch traced here: 106 us
  starting transfers between devices  70.8 us (66%)
  waiting for transfers between devices  20.2 us (19%)
  Pallas kernels  5.96 us (6%)
  matrix products  3.76 us (4%)
  other arithmetic  3.04 us (3%)
  local copies, waits for them, and re-layouts  1.79 us (2%)
    ppermute x12, starting transfers between devices, shift(): lax.ppermute(value, axis, [(i, (i + step) % size) for i in range(size)])  56.5 us
    all_to_all x2, starting transfers between devices, exchange(): return lax.all_to_all(value, axis, 0, 0, tiled=True)  14.3 us
    ppermute x12, waiting for transfers between devices, shift(): lax.ppermute(value, axis, [(i, (i + step) % size) for i in range(size)])  14.1 us
    all_to_all x2, waiting for transfers between devices, exchange(): return lax.all_to_all(value, axis, 0, 0, tiled=True)  6.08 us
    pallas_call x4, Pallas kernels, whole(): pl.pallas_call(kernel, out_shape=outs, in_specs=[SMEM] + [VMEM] * len(arg...  5.96 us
    dot_general x1, matrix products, body(): lax.dot_general(hidden_all, cotangent, (((0,), (0,)), ((), ())), preferre...  3.76 us
  transfers between devices with their start and end apart: 14, of which 5 were waited for; matrix products, arithmetic and copies ran while one was open for 5% of the time, Pallas kernels for 4%

profile of v4, /device:TPU:136, one launch (start us, length us, event | category | flops | bytes accessed | tf_op | source)
XLA Modules:
  0.0 106.5 jit_solution(10781695493932587731)
XLA Ops:
  0.6 0.0 copy-start
  0.6 1.2 %fusion = bf16[32,1792]{1,0:T(8,128)(2,1)S(1)} fusion(bf16[32,1792]{1,0:T(8,128)(2,1)} %param.5, bf16[32,1792]{1,0:T(8,128)(2,1)} %param.4), kind=kLoop, calls=%fused_computation.7 | loop fusion | flops 458752 | bytes 344064 | tf_op jit(solution)/shard_map/convert_element_type | solution.py:116
  1.8 10.9 %collective-permute-start.1 = (bf16[32,1792]{1,0:T(8,128)(2,1)S(1)}, bf16[32,1792]{1,0:T(8,128)(2,1)S(1)}, u32[]{:S(2)}, u32[]{:S(2)}) collective-permute-start(bf16[32,1792]{1,0:T(8,128)(2,1)S(1)} %fusion), channel_id=1, source_target_pairs={{0,4},{4,8},{8,0},{1,5},{5,9},{9,1},{2,6},{6,10},{10,2},{3,7},{7,1... | collective-permute-start | bytes 344072 | tf_op jit(solution)/shard_map/ppermute | solution.py:18
  12.7 3.8 %collective-permute-start = (bf16[32,1792]{1,0:T(8,128)(2,1)S(1)}, bf16[32,1792]{1,0:T(8,128)(2,1)S(1)}, u32[]{:S(2)}, u32[]{:S(2)}) collective-permute-start(bf16[32,1792]{1,0:T(8,128)(2,1)S(1)} %fusion), channel_id=1, source_target_pairs={{0,8},{4,0},{8,4},{1,9},{5,1},{9,5},{2,10},{6,2},{10,6},{3,11},{7,... | collective-permute-start | bytes 344072 | tf_op jit(solution)/shard_map/ppermute | solution.py:18
  16.5 0.1 pad_add_fusion.place
  16.6 1.0 copy-done.1
  17.6 1.3 %shard_map.75 = bf16[12,32,512]{2,1,0:T(8,128)(2,1)} custom-call(s32[2]{0:T(128)S(1)} %pad_add_fusion.place, bf16[32,6144]{1,0:T(8,128)(2,1)S(1)} %copy-done.1), custom_call_target="tpu_custom_call" | custom-call | bytes 1048576 | tf_op jit(solution)/shard_map/pallas_call | solution.py:38
  18.9 3.8 %collective-permute-done.1 = bf16[32,1792]{1,0:T(8,128)(2,1)S(1)} collective-permute-done((bf16[32,1792]{1,0:T(8,128)(2,1)S(1)}, bf16[32,1792]{1,0:T(8,128)(2,1)S(1)}, u32[]{:S(2)}, u32[]{:S(2)}) %collective-permute-start.1) | collective-permute-done | bytes 114720 | tf_op jit(solution)/shard_map/ppermute | solution.py:18
  22.7 6.2 %collective-permute-done = bf16[32,1792]{1,0:T(8,128)(2,1)S(1)} collective-permute-done((bf16[32,1792]{1,0:T(8,128)(2,1)S(1)}, bf16[32,1792]{1,0:T(8,128)(2,1)S(1)}, u32[]{:S(2)}, u32[]{:S(2)}) %collective-permute-start) | collective-permute-done | bytes 114720 | tf_op jit(solution)/shard_map/ppermute | solution.py:18
  29.0 8.2 %all-to-all-start = ((bf16[12,32,512]{2,1,0:T(8,128)(2,1)}), bf16[12,32,512]{2,1,0:T(8,128)(2,1)S(1)}, u32[]{:S(2)}, u32[]{:S(2)}) async-start(bf16[12,32,512]{2,1,0:T(8,128)(2,1)} %shard_map.75), calls=%async_computation | async-start | bytes 786432 | tf_op jit(solution)/shard_map/all_to_all | solution.py:26
  37.2 3.9 %collective-permute-start.7 = (bf16[96,1792]{1,0:T(8,128)(2,1)S(1)}, bf16[96,1792]{1,0:T(8,128)(2,1)S(1)}, u32[]{:S(2)}, u32[]{:S(2)}) collective-permute-start(bf16[96,1792]{1,0:T(8,128)(2,1)S(1)} %constant_dynamic-update-slice_fusion.own), channel_id=1, source_target_pairs={{0,1},{1,2},{2,3},{3,0},{4,5},{5,6},{6,7},{7,4},{8,9},{9,10},{10,1... | collective-permute-start | bytes 1032200 | tf_op jit(solution)/shard_map/ppermute | solution.py:18
  41.1 4.6 %collective-permute-start.6 = (bf16[96,1792]{1,0:T(8,128)(2,1)S(1)}, bf16[96,1792]{1,0:T(8,128)(2,1)S(1)}, u32[]{:S(2)}, u32[]{:S(2)}) collective-permute-start(bf16[96,1792]{1,0:T(8,128)(2,1)S(1)} %constant_dynamic-update-slice_fusion.own), channel_id=1, source_target_pairs={{0,2},{1,3},{2,0},{3,1},{4,6},{5,7},{6,4},{7,5},{8,10},{9,11},{10,... | collective-permute-start | bytes 1032200 | tf_op jit(solution)/shard_map/ppermute | solution.py:18
  45.7 3.4 %collective-permute-start.5 = (bf16[96,1792]{1,0:T(8,128)(2,1)S(1)}, bf16[96,1792]{1,0:T(8,128)(2,1)}, u32[]{:S(2)}, u32[]{:S(2)}) collective-permute-start(bf16[96,1792]{1,0:T(8,128)(2,1)S(1)} %constant_dynamic-update-slice_fusion.own), channel_id=1, source_target_pairs={{0,3},{1,0},{2,1},{3,2},{4,7},{5,4},{6,5},{7,6},{8,11},{9,8},{10,9... | collective-permute-start | bytes 1032200 | tf_op jit(solution)/shard_map/ppermute | solution.py:18
  49.1 3.3 %all-to-all-done.got = bf16[12,32,512]{2,1,0:T(8,128)(2,1)S(1)} async-done(((bf16[12,32,512]{2,1,0:T(8,128)(2,1)}), bf16[12,32,512]{2,1,0:T(8,128)(2,1)S(1)}, u32[]{:S(2)}, u32[]{:S(2)}) %all-to-all-start) | async-done | bytes 393248 | tf_op jit(solution)/shard_map/all_to_all | solution.py:26
  52.4 0.0 copy-done
  52.4 1.5 %shard_map.76 = (bf16[96,1792]{1,0:T(8,128)(2,1)S(1)}, bf16[96,1792]{1,0:T(8,128)(2,1)S(1)}, bf16[96,1792]{1,0:T(8,128)(2,1)S(1)}, bf16[96,1792]{1,0:T(8,128)(2,1)S(1)}, bf16[384,512]{1,0:T(8,128)(2,1)S(1)}) custom-call(s32[2]{0:T(128)S(1)} %pad_add_fusion.place, bf16[12,32,512]{2,1,0:T(8,128)(2,1)S(1)} %all-to-all-done.got, bf16[1792,512]{1,0:T(8,128)(2,1)S(1)} %copy-done), custom_call_target="tpu_custom_call" | custom-call | flops 704643072 | bytes 104857600 | tf_op jit(solution)/shard_map/pallas_call | solution.py:38
  53.9 0.0 copy-start.3
  53.9 0.7 copy-done.3
  54.6 2.5 %collective-permute-start.2 = (bf16[96,1792]{1,0:T(8,128)(2,1)S(1)}, bf16[96,1792]{1,0:T(8,128)(2,1)S(1)}, u32[]{:S(2)}, u32[]{:S(2)}) collective-permute-start(bf16[96,1792]{1,0:T(8,128)(2,1)S(1)} %get-tuple-element.33), channel_id=1, source_target_pairs={{0,1},{1,2},{2,3},{3,0},{4,5},{5,6},{6,7},{7,4},{8,9},{9,10},{10,1... | collective-permute-start | bytes 1032200 | tf_op jit(solution)/shard_map/ppermute | solution.py:18
  57.1 4.0 %collective-permute-start.3 = (bf16[96,1792]{1,0:T(8,128)(2,1)S(1)}, bf16[96,1792]{1,0:T(8,128)(2,1)S(1)}, u32[]{:S(2)}, u32[]{:S(2)}) collective-permute-start(bf16[96,1792]{1,0:T(8,128)(2,1)S(1)} %get-tuple-element.34), channel_id=1, source_target_pairs={{0,2},{1,3},{2,0},{3,1},{4,6},{5,7},{6,4},{7,5},{8,10},{9,11},{10,... | collective-permute-start | bytes 1032200 | tf_op jit(solution)/shard_map/ppermute | solution.py:18
  61.1 0.0 collective-permute-done.7.third
  61.1 2.5 %collective-permute-start.4 = (bf16[96,1792]{1,0:T(8,128)(2,1)S(1)}, bf16[96,1792]{1,0:T(8,128)(2,1)S(1)}, u32[]{:S(2)}, u32[]{:S(2)}) collective-permute-start(bf16[96,1792]{1,0:T(8,128)(2,1)S(1)} %get-tuple-element.35), channel_id=1, source_target_pairs={{0,3},{1,0},{2,1},{3,2},{4,7},{5,4},{6,5},{7,6},{8,11},{9,8},{10,9... | collective-permute-start | bytes 1032200 | tf_op jit(solution)/shard_map/ppermute | solution.py:18
  63.6 0.0 collective-permute-done.6.second
  63.7 0.0 collective-permute-done.5.first
  63.7 1.9 %shard_map.77 = (bf16[4,32,512]{2,1,0:T(8,128)(2,1)S(1)}, bf16[4,32,512]{2,1,0:T(8,128)(2,1)S(1)}, bf16[4,32,512]{2,1,0:T(8,128)(2,1)S(1)}, bf16[384,1792]{1,0:T(8,128)(2,1)S(1)}) custom-call(s32[2]{0:T(128)S(1)} %pad_add_fusion.place, bf16[96,1792]{1,0:T(8,128)(2,1)S(1)} %constant_dynamic-update-slice_fusion.own, ...), custom_call_target="tpu_custom_call" | custom-call | flops 704643072 | bytes 4194304 | tf_op jit(solution)/shard_map/pallas_call | solution.py:38
  65.5 0.0 copy-start.2
  65.5 0.0 copy-start.4
  65.6 8.4 %collective-permute-start.8 = (bf16[4,32,512]{2,1,0:T(8,128)(2,1)S(1)}, bf16[4,32,512]{2,1,0:T(8,128)(2,1)S(1)}, u32[]{:S(2)}, u32[]{:S(2)}) collective-permute-start(bf16[4,32,512]{2,1,0:T(8,128)(2,1)S(1)} %get-tuple-element.44), channel_id=1, source_target_pairs={{0,8},{4,0},{8,4},{1,9},{5,1},{9,5},{2,10},{6,2},{10,6},{3,11},{7,... | collective-permute-start | bytes 393224 | tf_op jit(solution)/shard_map/ppermute | solution.py:18
  73.9 2.9 %collective-permute-start.9 = (bf16[4,32,512]{2,1,0:T(8,128)(2,1)S(1)}, bf16[4,32,512]{2,1,0:T(8,128)(2,1)S(1)}, u32[]{:S(2)}, u32[]{:S(2)}) collective-permute-start(bf16[4,32,512]{2,1,0:T(8,128)(2,1)S(1)} %get-tuple-element.45), channel_id=1, source_target_pairs={{0,4},{4,8},{8,0},{1,5},{5,9},{9,1},{2,6},{6,10},{10,2},{3,7},{7,1... | collective-permute-start | bytes 393224 | tf_op jit(solution)/shard_map/ppermute | solution.py:18
  76.9 0.0 collective-permute-done.2
  76.9 0.0 collective-permute-done.3
  76.9 0.0 collective-permute-done.4
  76.9 0.2 add_convert_fusion
  77.1 0.0 copy-done.2
  77.1 7.8 %collective-permute-start.10 = (bf16[32,1792]{1,0:T(8,128)(2,1)S(1)}, bf16[32,1792]{1,0:T(8,128)(2,1)S(1)}, u32[]{:S(2)}, u32[]{:S(2)}) collective-permute-start(bf16[32,1792]{1,0:T(8,128)(2,1)S(1)} %get-tuple-element.47), channel_id=1, source_target_pairs={{0,4},{4,8},{8,0},{1,5},{5,9},{9,1},{2,6},{6,10},{10,2},{3,7},{7,1... | collective-permute-start | bytes 344072 | tf_op jit(solution)/shard_map/ppermute | solution.py:18
  84.9 1.9 %collective-permute-start.11 = (bf16[32,1792]{1,0:T(8,128)(2,1)S(1)}, bf16[32,1792]{1,0:T(8,128)(2,1)S(1)}, u32[]{:S(2)}, u32[]{:S(2)}) collective-permute-start(bf16[32,1792]{1,0:T(8,128)(2,1)S(1)} %get-tuple-element.48), channel_id=1, source_target_pairs={{0,8},{4,0},{8,4},{1,9},{5,1},{9,5},{2,10},{6,2},{10,6},{3,11},{7,... | collective-permute-start | bytes 344072 | tf_op jit(solution)/shard_map/ppermute | solution.py:18
  86.8 0.0 collective-permute-done.8
  86.9 4.0 %collective-permute-done.9 = bf16[4,32,512]{2,1,0:T(8,128)(2,1)S(1)} collective-permute-done((bf16[4,32,512]{2,1,0:T(8,128)(2,1)S(1)}, bf16[4,32,512]{2,1,0:T(8,128)(2,1)S(1)}, u32[]{:S(2)}, u32[]{:S(2)}) %collective-permute-start.9) | collective-permute-done | bytes 131104 | tf_op jit(solution)/shard_map/ppermute | solution.py:18
  90.9 0.8 pad_maximum_fusion
  91.7 6.1 %all-to-all-start.1 = ((bf16[4,3,32,512]{3,2,1,0:T(8,128)(2,1)}), bf16[4,3,32,512]{3,2,1,0:T(8,128)(2,1)S(1)}, u32[]{:S(2)}, u32[]{:S(2)}) async-start(bf16[4,3,32,512]{3,2,1,0:T(8,128)(2,1)} %pad_maximum_fusion), calls=%async_computation.1 | async-start | bytes 786432 | tf_op jit(solution)/shard_map/all_to_all | solution.py:26
  97.8 0.0 copy-done.4
  97.8 3.8 %convolution_convert_fusion = bf16[1792,512]{1,0:T(8,128)(2,1)} fusion(bf16[384,1792]{1,0:T(8,128)(2,1)} %copy-done.2, bf16[384,512]{1,0:T(8,128)(2,1)S(1)} %copy-done.4), kind=kOutput, calls=%fused_computation | convolution fusion | flops 705560576 | bytes 3604480 | tf_op jit(solution)/shard_map/dot_general | solution.py:155
  101.6 0.0 collective-permute-done.10
  101.6 0.0 collective-permute-done.11
  101.6 0.0 copy-done.5
  101.6 0.8 multiply_convert_fusion
  102.4 2.8 %all-to-all-done.1.columns = bf16[4,3,32,512]{3,2,1,0:T(8,128)(2,1)S(1)} async-done(((bf16[4,3,32,512]{3,2,1,0:T(8,128)(2,1)}), bf16[4,3,32,512]{3,2,1,0:T(8,128)(2,1)S(1)}, u32[]{:S(2)}, u32[]{:S(2)}) %all-to-all-start.1) | async-done | bytes 393248 | tf_op jit(solution)/shard_map/all_to_all | solution.py:26
  105.2 1.3 %shard_map.78 = bf16[32,6144]{1,0:T(8,128)(2,1)} custom-call(s32[2]{0:T(128)S(1)} %pad_add_fusion.place, bf16[4,3,32,512]{3,2,1,0:T(8,128)(2,1)S(1)} %all-to-all-done.1.columns), custom_call_target="tpu_custom_call" | custom-call | bytes 1048576 | tf_op jit(solution)/shard_map/pallas_call | solution.py:38
  (7 shorter events, 0.0 us)
Async XLA Ops:
  0.6 51.8 %copy-start = (bf16[1792,512]{1,0:T(8,128)(2,1)S(1)}, bf16[1792,512]{1,0:T(8,128)(2,1)}, u32[]{:S(2)}) copy-start(bf16[1792,512]{1,0:T(8,128)(2,1)} %weight.3) | copy-start | bytes 5505028
  1.8 20.9 %collective-permute-start.1 = (bf16[32,1792]{1,0:T(8,128)(2,1)S(1)}, bf16[32,1792]{1,0:T(8,128)(2,1)S(1)}, u32[]{:S(2)}, u32[]{:S(2)}) collective-permute-start(bf16[32,1792]{1,0:T(8,128)(2,1)S(1)} %fusion), channel_id=1, source_target_pairs={{0,4},{4,8},{8,0},{1,5},{5,9},{9,1},{2,6},{6,10},{10,2},{3,7},{7,1... | collective-permute-start | bytes 344072 | tf_op jit(solution)/shard_map/ppermute | solution.py:18
  12.7 16.2 %collective-permute-start = (bf16[32,1792]{1,0:T(8,128)(2,1)S(1)}, bf16[32,1792]{1,0:T(8,128)(2,1)S(1)}, u32[]{:S(2)}, u32[]{:S(2)}) collective-permute-start(bf16[32,1792]{1,0:T(8,128)(2,1)S(1)} %fusion), channel_id=1, source_target_pairs={{0,8},{4,0},{8,4},{1,9},{5,1},{9,5},{2,10},{6,2},{10,6},{3,11},{7,... | collective-permute-start | bytes 344072 | tf_op jit(solution)/shard_map/ppermute | solution.py:18
  16.6 1.0 copy-start.1
  29.0 23.4 %all-to-all-start = ((bf16[12,32,512]{2,1,0:T(8,128)(2,1)}), bf16[12,32,512]{2,1,0:T(8,128)(2,1)S(1)}, u32[]{:S(2)}, u32[]{:S(2)}) async-start(bf16[12,32,512]{2,1,0:T(8,128)(2,1)} %shard_map.75), calls=%async_computation | async-start | bytes 786432 | tf_op jit(solution)/shard_map/all_to_all | solution.py:26
  37.2 23.9 %collective-permute-start.7 = (bf16[96,1792]{1,0:T(8,128)(2,1)S(1)}, bf16[96,1792]{1,0:T(8,128)(2,1)S(1)}, u32[]{:S(2)}, u32[]{:S(2)}) collective-permute-start(bf16[96,1792]{1,0:T(8,128)(2,1)S(1)} %constant_dynamic-update-slice_fusion.own), channel_id=1, source_target_pairs={{0,1},{1,2},{2,3},{3,0},{4,5},{5,6},{6,7},{7,4},{8,9},{9,10},{10,1... | collective-permute-start | bytes 1032200 | tf_op jit(solution)/shard_map/ppermute | solution.py:18
  41.1 22.5 %collective-permute-start.6 = (bf16[96,1792]{1,0:T(8,128)(2,1)S(1)}, bf16[96,1792]{1,0:T(8,128)(2,1)S(1)}, u32[]{:S(2)}, u32[]{:S(2)}) collective-permute-start(bf16[96,1792]{1,0:T(8,128)(2,1)S(1)} %constant_dynamic-update-slice_fusion.own), channel_id=1, source_target_pairs={{0,2},{1,3},{2,0},{3,1},{4,6},{5,7},{6,4},{7,5},{8,10},{9,11},{10,... | collective-permute-start | bytes 1032200 | tf_op jit(solution)/shard_map/ppermute | solution.py:18
  45.7 17.9 %collective-permute-start.5 = (bf16[96,1792]{1,0:T(8,128)(2,1)S(1)}, bf16[96,1792]{1,0:T(8,128)(2,1)}, u32[]{:S(2)}, u32[]{:S(2)}) collective-permute-start(bf16[96,1792]{1,0:T(8,128)(2,1)S(1)} %constant_dynamic-update-slice_fusion.own), channel_id=1, source_target_pairs={{0,3},{1,0},{2,1},{3,2},{4,7},{5,4},{6,5},{7,6},{8,11},{9,8},{10,9... | collective-permute-start | bytes 1032200 | tf_op jit(solution)/shard_map/ppermute | solution.py:18
  53.9 0.7 copy-start.3
  54.6 22.2 %collective-permute-start.2 = (bf16[96,1792]{1,0:T(8,128)(2,1)S(1)}, bf16[96,1792]{1,0:T(8,128)(2,1)S(1)}, u32[]{:S(2)}, u32[]{:S(2)}) collective-permute-start(bf16[96,1792]{1,0:T(8,128)(2,1)S(1)} %get-tuple-element.33), channel_id=1, source_target_pairs={{0,1},{1,2},{2,3},{3,0},{4,5},{5,6},{6,7},{7,4},{8,9},{9,10},{10,1... | collective-permute-start | bytes 1032200 | tf_op jit(solution)/shard_map/ppermute | solution.py:18
  57.1 19.8 %collective-permute-start.3 = (bf16[96,1792]{1,0:T(8,128)(2,1)S(1)}, bf16[96,1792]{1,0:T(8,128)(2,1)S(1)}, u32[]{:S(2)}, u32[]{:S(2)}) collective-permute-start(bf16[96,1792]{1,0:T(8,128)(2,1)S(1)} %get-tuple-element.34), channel_id=1, source_target_pairs={{0,2},{1,3},{2,0},{3,1},{4,6},{5,7},{6,4},{7,5},{8,10},{9,11},{10,... | collective-permute-start | bytes 1032200 | tf_op jit(solution)/shard_map/ppermute | solution.py:18
  61.1 15.8 %collective-permute-start.4 = (bf16[96,1792]{1,0:T(8,128)(2,1)S(1)}, bf16[96,1792]{1,0:T(8,128)(2,1)S(1)}, u32[]{:S(2)}, u32[]{:S(2)}) collective-permute-start(bf16[96,1792]{1,0:T(8,128)(2,1)S(1)} %get-tuple-element.35), channel_id=1, source_target_pairs={{0,3},{1,0},{2,1},{3,2},{4,7},{5,4},{6,5},{7,6},{8,11},{9,8},{10,9... | collective-permute-start | bytes 1032200 | tf_op jit(solution)/shard_map/ppermute | solution.py:18
  65.5 11.5 %copy-start.2 = (bf16[384,1792]{1,0:T(8,128)(2,1)}, bf16[384,1792]{1,0:T(8,128)(2,1)S(1)}, u32[]{:S(2)}) copy-start(bf16[384,1792]{1,0:T(8,128)(2,1)S(1)} %get-tuple-element.52) | copy-start | bytes 4128772
  65.5 32.3 %copy-start.4 = (bf16[384,512]{1,0:T(8,128)(2,1)S(1)}, bf16[384,512]{1,0:T(8,128)(2,1)}, u32[]{:S(2)}) copy-start(bf16[384,512]{1,0:T(8,128)(2,1)} %copy-done.3) | copy-start | bytes 1179652
  65.6 21.3 %collective-permute-start.8 = (bf16[4,32,512]{2,1,0:T(8,128)(2,1)S(1)}, bf16[4,32,512]{2,1,0:T(8,128)(2,1)S(1)}, u32[]{:S(2)}, u32[]{:S(2)}) collective-permute-start(bf16[4,32,512]{2,1,0:T(8,128)(2,1)S(1)} %get-tuple-element.44), channel_id=1, source_target_pairs={{0,8},{4,0},{8,4},{1,9},{5,1},{9,5},{2,10},{6,2},{10,6},{3,11},{7,... | collective-permute-start | bytes 393224 | tf_op jit(solution)/shard_map/ppermute | solution.py:18
  73.9 16.9 %collective-permute-start.9 = (bf16[4,32,512]{2,1,0:T(8,128)(2,1)S(1)}, bf16[4,32,512]{2,1,0:T(8,128)(2,1)S(1)}, u32[]{:S(2)}, u32[]{:S(2)}) collective-permute-start(bf16[4,32,512]{2,1,0:T(8,128)(2,1)S(1)} %get-tuple-element.45), channel_id=1, source_target_pairs={{0,4},{4,8},{8,0},{1,5},{5,9},{9,1},{2,6},{6,10},{10,2},{3,7},{7,1... | collective-permute-start | bytes 393224 | tf_op jit(solution)/shard_map/ppermute | solution.py:18
  77.1 24.5 %collective-permute-start.10 = (bf16[32,1792]{1,0:T(8,128)(2,1)S(1)}, bf16[32,1792]{1,0:T(8,128)(2,1)S(1)}, u32[]{:S(2)}, u32[]{:S(2)}) collective-permute-start(bf16[32,1792]{1,0:T(8,128)(2,1)S(1)} %get-tuple-element.47), channel_id=1, source_target_pairs={{0,4},{4,8},{8,0},{1,5},{5,9},{9,1},{2,6},{6,10},{10,2},{3,7},{7,1... | collective-permute-start | bytes 344072 | tf_op jit(solution)/shard_map/ppermute | solution.py:18
  84.9 16.6 %collective-permute-start.11 = (bf16[32,1792]{1,0:T(8,128)(2,1)S(1)}, bf16[32,1792]{1,0:T(8,128)(2,1)S(1)}, u32[]{:S(2)}, u32[]{:S(2)}) collective-permute-start(bf16[32,1792]{1,0:T(8,128)(2,1)S(1)} %get-tuple-element.48), channel_id=1, source_target_pairs={{0,8},{4,0},{8,4},{1,9},{5,1},{9,5},{2,10},{6,2},{10,6},{3,11},{7,... | collective-permute-start | bytes 344072 | tf_op jit(solution)/shard_map/ppermute | solution.py:18
  91.7 13.5 %all-to-all-start.1 = ((bf16[4,3,32,512]{3,2,1,0:T(8,128)(2,1)}), bf16[4,3,32,512]{3,2,1,0:T(8,128)(2,1)S(1)}, u32[]{:S(2)}, u32[]{:S(2)}) async-start(bf16[4,3,32,512]{3,2,1,0:T(8,128)(2,1)} %pad_maximum_fusion), calls=%async_computation.1 | async-start | bytes 786432 | tf_op jit(solution)/shard_map/all_to_all | solution.py:26
  97.8 3.8 %copy-start.5 = (bf16[32,1792]{1,0:T(8,128)(2,1)S(1)}, bf16[32,1792]{1,0:T(8,128)(2,1)}, u32[]{:S(2)}) copy-start(bf16[32,1792]{1,0:T(8,128)(2,1)} %param.5) | copy-start | bytes 344068
  97.8 3.8 %copy-start.6 = (bf16[32,1792]{1,0:T(8,128)(2,1)S(1)}, bf16[32,1792]{1,0:T(8,128)(2,1)}, u32[]{:S(2)}) copy-start(bf16[32,1792]{1,0:T(8,128)(2,1)} %param.4) | copy-start | bytes 344068

commit v5 on v3

--- a/solution.py
+++ b/solution.py
@@ -10,6 +10,8 @@
 SUM_COST = 100 << 20
 GROUP = ("plane", "line")
 VMEM = pl.BlockSpec(memory_space=pltpu.VMEM)
+ANY = pl.BlockSpec(memory_space=pl.ANY)
+HBM = pl.BlockSpec(memory_space=pltpu.HBM)
 SMEM = pl.BlockSpec(memory_space=pltpu.SMEM)
 CHUNK = 256
 
@@ -34,12 +36,12 @@
     return sum(t.astype(jnp.float32) for t in terms)
 
 
-def whole(kernel, place, args, outs, scratch=(), flops=0, moved=1 << 20):
+def whole(kernel, place, args, outs, ins=None, dests=None, scratch=(), flops=0, moved=1 << 20):
     return pl.pallas_call(
         kernel,
         out_shape=outs,
-        in_specs=[SMEM] + [VMEM] * len(args),
-        out_specs=jax.tree.map(lambda _: VMEM, outs),
+        in_specs=[SMEM] + (ins or [VMEM] * len(args)),
+        out_specs=dests or jax.tree.map(lambda _: VMEM, outs),
         scratch_shapes=list(scratch),
         compiler_params=pltpu.CompilerParams(vmem_limit_bytes=24 << 20),
         cost_estimate=pl.CostEstimate(flops=flops, bytes_accessed=moved, transcendentals=0),
@@ -52,7 +54,7 @@
         blocks[b] = rows[:, b * width : (b + 1) * width]
 
 
-def partial_kernel(place, got, weight, stay, first, second, third, ordered):
+def partial_kernel(place, got, weight, stay, first, second, third, kept, ordered, sem):
     rows = got.shape[1]
     held = PLANES * rows
     line = ordered.shape[0] // held
@@ -61,6 +63,8 @@
             at = k * held + j * rows
             source = lax.rem(place[0] + j, PLANES) * line + lax.rem(place[1] + k, line)
             ordered[at : at + rows, :] = got[source]
+    keep = pltpu.make_async_copy(ordered, kept, sem)
+    keep.start()
     for c in range(weight.shape[0] // CHUNK):
         span = slice(c * CHUNK, (c + 1) * CHUNK)
         part = lax.dot_general(
@@ -71,14 +75,23 @@
         ).astype(jnp.bfloat16)
         for k, piece in enumerate((stay, first, second, third)):
             piece[:, span] = part[k * held : (k + 1) * held]
+    keep.wait()
 
 
-def column_kernel(place, own, first, second, third, weight, columns, every):
+def column_kernel(place, own, first, second, third, weight, columns, kept, every, sems):
     rows = columns.shape[1]
     held = PLANES * rows
     line = every.shape[0] // held
-    for k, piece in enumerate((own, first, second, third)):
-        every[k * held : (k + 1) * held, :] = piece[...]
+    copies = [
+        pltpu.make_async_copy(piece, every.at[pl.ds(k * held, held)], sems.at[k])
+        for k, piece in enumerate((own, first, second, third))
+    ]
+    for copy in copies:
+        copy.start()
+    for copy in copies:
+        copy.wait()
+    keep = pltpu.make_async_copy(every, kept, sems.at[line])
+    keep.start()
     for c in range(weight.shape[1] // CHUNK):
         span = slice(c * CHUNK, (c + 1) * CHUNK)
         part = jnp.dot(
@@ -89,6 +102,7 @@
                 at = k * held + j * rows
                 owner = lax.rem(place[0] + j, PLANES) * line + lax.rem(place[1] + k, line)
                 columns[owner, :, span] = part[at : at + rows]
+    keep.wait()
 
 
 def output_kernel(place, columns, output):
@@ -128,6 +142,8 @@
         place,
         [got, down_weight],
         [made(PLANES * rows, hidden_width)] * line + [made(group * rows, width)],
+        dests=[VMEM] * line + [HBM],
+        scratch=[pltpu.VMEM((group * rows, width), jnp.bfloat16), pltpu.SemaphoreType.DMA],
         flops=2 * group * rows * width * hidden_width,
         moved=SUM_COST,
     )
@@ -144,6 +160,12 @@
         place,
         [mine, *by_line, down_weight],
         [made(group, rows, width), made(group * rows, hidden_width)],
+        ins=[ANY] * line + [VMEM],
+        dests=[VMEM, HBM],
+        scratch=[
+            pltpu.VMEM((group * rows, hidden_width), jnp.bfloat16),
+            pltpu.SemaphoreType.DMA((line + 1,)),
+        ],
         flops=2 * group * rows * width * hidden_width,
         moved=4 << 20,
     )

time: 108 us -> 107 us (level)
  waiting for transfers between devices: 25.4 us -> 23.7 us
  starting transfers between devices: 64.7 us -> 63.5 us
  Pallas kernels: 7.7 us -> 8.88 us
    ppermute x10, waiting for transfers between devices: 19 us -> 17.4 us  [shift(): lax.ppermute(value, axis, [(i, (i + step) % size) for i in range(size)])]
    all_to_all x2, starting transfers between devices: 20.8 us -> 19.5 us  [exchange(): return lax.all_to_all(value, axis, 0, 0, tiled=True)]
    pallas_call x4, Pallas kernels: 7.7 us -> 8.88 us  [whole(): pl.pallas_call(kernel, out_shape=outs, in_specs=[SMEM] + (ins or [VMEM] *...]
  transfers between devices with their start and end apart: 12 -> 12, of which waited for: 4 -> 4; matrix products, arithmetic and copies ran while one was open for 4% -> 5% of each run, Pallas kernels for 6% -> 7%
where the time goes in v5:
time: 107 us; the launch traced here: 106 us
  starting transfers between devices  63.5 us (59%)
  waiting for transfers between devices  23.7 us (22%)
  Pallas kernels  8.88 us (8%)
  other arithmetic  3.54 us (3%)
  local copies, waits for them, and re-layouts  2.85 us (3%)
  matrix products  2.37 us (2%)
    ppermute x10, starting transfers between devices, shift(): lax.ppermute(value, axis, [(i, (i + step) % size) for i in range(size)])  43.9 us
    all_to_all x2, starting transfers between devices, exchange(): return lax.all_to_all(value, axis, 0, 0, tiled=True)  19.5 us
    ppermute x10, waiting for transfers between devices, shift(): lax.ppermute(value, axis, [(i, (i + step) % size) for i in range(size)])  17.4 us
    pallas_call x4, Pallas kernels, whole(): pl.pallas_call(kernel, out_shape=outs, in_specs=[SMEM] + (ins or [VMEM] *...  8.88 us
    all_to_all x2, waiting for transfers between devices, exchange(): return lax.all_to_all(value, axis, 0, 0, tiled=True)  6.37 us
    unnamed x18, local copies, waits for them, and re-layouts  2.84 us
    dot_general x1, matrix products, body(): lax.dot_general(hidden_all, cotangent, (((0,), (0,)), ((), ())), preferre...  2.37 us
  transfers between devices with their start and end apart: 12, of which 4 were waited for; matrix products, arithmetic and copies ran while one was open for 5% of the time, Pallas kernels for 7%

profile of v5, /device:TPU:6, one launch (start us, length us, event | category | flops | bytes accessed | tf_op | source)
XLA Modules:
  0.0 105.7 jit_solution(5350963290148311939)
XLA Ops:
  0.6 0.0 copy-start
  0.6 1.2 %fusion = bf16[32,1792]{1,0:T(8,128)(2,1)S(1)} fusion(bf16[32,1792]{1,0:T(8,128)(2,1)} %param.5, bf16[32,1792]{1,0:T(8,128)(2,1)} %param.4), kind=kLoop, calls=%fused_computation.6 | loop fusion | flops 458752 | bytes 344064 | tf_op jit(solution)/shard_map/convert_element_type | solution.py:128
  1.8 10.9 %collective-permute-start.1 = (bf16[32,1792]{1,0:T(8,128)(2,1)S(1)}, bf16[32,1792]{1,0:T(8,128)(2,1)S(1)}, u32[]{:S(2)}, u32[]{:S(2)}) collective-permute-start(bf16[32,1792]{1,0:T(8,128)(2,1)S(1)} %fusion), channel_id=1, source_target_pairs={{0,4},{4,8},{8,0},{1,5},{5,9},{9,1},{2,6},{6,10},{10,2},{3,7},{7,1... | collective-permute-start | bytes 344072 | tf_op jit(solution)/shard_map/ppermute | solution.py:20
  12.7 5.6 %collective-permute-start = (bf16[32,1792]{1,0:T(8,128)(2,1)S(1)}, bf16[32,1792]{1,0:T(8,128)(2,1)S(1)}, u32[]{:S(2)}, u32[]{:S(2)}) collective-permute-start(bf16[32,1792]{1,0:T(8,128)(2,1)S(1)} %fusion), channel_id=1, source_target_pairs={{0,8},{4,0},{8,4},{1,9},{5,1},{9,5},{2,10},{6,2},{10,6},{3,11},{7,... | collective-permute-start | bytes 344072 | tf_op jit(solution)/shard_map/ppermute | solution.py:20
  18.3 0.1 pad_add_fusion.place
  18.4 0.0 copy-start.1
  18.4 1.0 copy-done.1
  19.4 1.3 %shard_map.75 = bf16[12,32,512]{2,1,0:T(8,128)(2,1)} custom-call(s32[2]{0:T(128)S(1)} %pad_add_fusion.place, bf16[32,6144]{1,0:T(8,128)(2,1)S(1)} %copy-done.1), custom_call_target="tpu_custom_call" | custom-call | bytes 1048576 | tf_op jit(solution)/shard_map/pallas_call | solution.py:40
  20.7 0.0 collective-permute-done.1
  20.7 9.3 %collective-permute-done = bf16[32,1792]{1,0:T(8,128)(2,1)S(1)} collective-permute-done((bf16[32,1792]{1,0:T(8,128)(2,1)S(1)}, bf16[32,1792]{1,0:T(8,128)(2,1)S(1)}, u32[]{:S(2)}, u32[]{:S(2)}) %collective-permute-start) | collective-permute-done | bytes 114720 | tf_op jit(solution)/shard_map/ppermute | solution.py:20
  30.0 11.4 %all-to-all-start = ((bf16[12,32,512]{2,1,0:T(8,128)(2,1)}), bf16[12,32,512]{2,1,0:T(8,128)(2,1)S(1)}, u32[]{:S(2)}, u32[]{:S(2)}) async-start(bf16[12,32,512]{2,1,0:T(8,128)(2,1)} %shard_map.75), calls=%async_computation | async-start | bytes 786432 | tf_op jit(solution)/shard_map/all_to_all | solution.py:28
  41.4 2.0 %collective-permute-start.4 = (bf16[96,1792]{1,0:T(8,128)(2,1)S(1)}, bf16[96,1792]{1,0:T(8,128)(2,1)S(1)}, u32[]{:S(2)}, u32[]{:S(2)}) collective-permute-start(bf16[96,1792]{1,0:T(8,128)(2,1)S(1)} %constant_dynamic-update-slice_fusion.own), channel_id=1, source_target_pairs={{0,1},{1,2},{2,3},{3,0},{4,5},{5,6},{6,7},{7,4},{8,9},{9,10},{10,1... | collective-permute-start | bytes 1032200 | tf_op jit(solution)/shard_map/ppermute | solution.py:20
  43.4 4.8 %collective-permute-start.3 = (bf16[96,1792]{1,0:T(8,128)(2,1)S(1)}, bf16[96,1792]{1,0:T(8,128)(2,1)}, u32[]{:S(2)}, u32[]{:S(2)}) collective-permute-start(bf16[96,1792]{1,0:T(8,128)(2,1)S(1)} %constant_dynamic-update-slice_fusion.own), channel_id=1, source_target_pairs={{0,2},{1,3},{2,0},{3,1},{4,6},{5,7},{6,4},{7,5},{8,10},{9,11},{10,... | collective-permute-start | bytes 1032200 | tf_op jit(solution)/shard_map/ppermute | solution.py:20
  48.2 1.9 %collective-permute-start.2 = (bf16[96,1792]{1,0:T(8,128)(2,1)S(1)}, bf16[96,1792]{1,0:T(8,128)(2,1)}, u32[]{:S(2)}, u32[]{:S(2)}) collective-permute-start(bf16[96,1792]{1,0:T(8,128)(2,1)S(1)} %constant_dynamic-update-slice_fusion.own), channel_id=1, source_target_pairs={{0,3},{1,0},{2,1},{3,2},{4,7},{5,4},{6,5},{7,6},{8,11},{9,8},{10,9... | collective-permute-start | bytes 1032200 | tf_op jit(solution)/shard_map/ppermute | solution.py:20
  50.1 6.4 %all-to-all-done.got = bf16[12,32,512]{2,1,0:T(8,128)(2,1)S(1)} async-done(((bf16[12,32,512]{2,1,0:T(8,128)(2,1)}), bf16[12,32,512]{2,1,0:T(8,128)(2,1)S(1)}, u32[]{:S(2)}, u32[]{:S(2)}) %all-to-all-start) | async-done | bytes 393248 | tf_op jit(solution)/shard_map/all_to_all | solution.py:28
  56.5 0.0 copy-done
  56.5 2.7 %shard_map.76 = (bf16[96,1792]{1,0:T(8,128)(2,1)S(1)}, bf16[96,1792]{1,0:T(8,128)(2,1)}, bf16[96,1792]{1,0:T(8,128)(2,1)}, bf16[96,1792]{1,0:T(8,128)(2,1)}, bf16[384,512]{1,0:T(8,128)(2,1)S(1)}) custom-call(s32[2]{0:T(128)S(1)} %pad_add_fusion.place, bf16[12,32,512]{2,1,0:T(8,128)(2,1)S(1)} %all-to-all-done.got, bf16[1792,512]{1,0:T(8,128)(2,1)S(1)} %copy-done), custom_call_target="tpu_custom_call" | custom-call | flops 704643072 | bytes 104857600 | tf_op jit(solution)/shard_map/pallas_call | solution.py:40
  59.2 0.0 copy-start.4
  59.2 0.7 copy-done.4
  59.9 3.8 %collective-permute-start.5 = (bf16[96,1792]{1,0:T(8,128)(2,1)}, bf16[96,1792]{1,0:T(8,128)(2,1)}, u32[]{:S(2)}, u32[]{:S(2)}) collective-permute-start(bf16[96,1792]{1,0:T(8,128)(2,1)} %get-tuple-element.32), channel_id=1, source_target_pairs={{0,1},{1,2},{2,3},{3,0},{4,5},{5,6},{6,7},{7,4},{8,9},{9,10},{10,1... | collective-permute-start | bytes 1032200 | tf_op jit(solution)/shard_map/ppermute | solution.py:20
  63.7 1.9 %collective-permute-start.6 = (bf16[96,1792]{1,0:T(8,128)(2,1)}, bf16[96,1792]{1,0:T(8,128)(2,1)}, u32[]{:S(2)}, u32[]{:S(2)}) collective-permute-start(bf16[96,1792]{1,0:T(8,128)(2,1)} %get-tuple-element.33), channel_id=1, source_target_pairs={{0,2},{1,3},{2,0},{3,1},{4,6},{5,7},{6,4},{7,5},{8,10},{9,11},{10,... | collective-permute-start | bytes 1032200 | tf_op jit(solution)/shard_map/ppermute | solution.py:20
  65.7 0.0 collective-permute-done.4.third
  65.7 3.3 %collective-permute-start.7 = (bf16[96,1792]{1,0:T(8,128)(2,1)}, bf16[96,1792]{1,0:T(8,128)(2,1)}, u32[]{:S(2)}, u32[]{:S(2)}) collective-permute-start(bf16[96,1792]{1,0:T(8,128)(2,1)} %get-tuple-element.34), channel_id=1, source_target_pairs={{0,3},{1,0},{2,1},{3,2},{4,7},{5,4},{6,5},{7,6},{8,11},{9,8},{10,9... | collective-permute-start | bytes 1032200 | tf_op jit(solution)/shard_map/ppermute | solution.py:20
  69.0 0.0 collective-permute-done.3.second
  69.0 0.0 collective-permute-done.2.first
  69.0 3.6 %shard_map.77 = (bf16[12,32,512]{2,1,0:T(8,128)(2,1)}, bf16[384,1792]{1,0:T(8,128)(2,1)S(1)}) custom-call(s32[2]{0:T(128)S(1)} %pad_add_fusion.place, bf16[96,1792]{1,0:T(8,128)(2,1)S(1)} %constant_dynamic-update-slice_fusion.own, bf16[96,1792]{1,0:T(8,128)(2,1)} %collective-permute-done.2.first, bf16[96,1792]{1,0:T(8,128)(2,1)} %collective-permute-done.3.second, ...), custom_call_target="tpu_custom_call" | custom-call | flops 704643072 | bytes 4194304 | tf_op jit(solution)/shard_map/pallas_call | solution.py:40
  72.6 0.0 copy-start.2
  72.6 1.1 %copy-done.2 = bf16[384,1792]{1,0:T(8,128)(2,1)} copy-done((bf16[384,1792]{1,0:T(8,128)(2,1)}, bf16[384,1792]{1,0:T(8,128)(2,1)S(1)}, u32[]{:S(2)}) %copy-start.2) | copy-done | bytes 1376280
  73.7 0.0 copy-start.5
  73.7 8.1 %all-to-all-start.1 = ((bf16[12,32,512]{2,1,0:T(8,128)(2,1)}), bf16[12,32,512]{2,1,0:T(8,128)(2,1)S(1)}, u32[]{:S(2)}, u32[]{:S(2)}) async-start(bf16[12,32,512]{2,1,0:T(8,128)(2,1)} %get-tuple-element.31), calls=%async_computation.1 | async-start | bytes 786432 | tf_op jit(solution)/shard_map/all_to_all | solution.py:28
  81.8 0.0 collective-permute-done.5
  81.8 0.0 collective-permute-done.6
  81.8 0.0 collective-permute-done.7
  81.9 1.5 %add_convert_fusion = (bf16[32,1792]{1,0:T(8,128)(2,1)S(1)}, bf16[32,1792]{1,0:T(8,128)(2,1)S(1)}, bf16[32,1792]{1,0:T(8,128)(2,1)S(1)}) fusion(bf16[96,1792]{1,0:T(8,128)(2,1)} %collective-permute-done.7, bf16[96,1792]{1,0:T(8,128)(2,1)} %collective-permute-done.6, bf16[96,1792]{1,0:T(8,128)(2,1)} %collective-permute-done.5, ...), kind=kLoop, calls=%fused_computation.16 | loop fusion | flops 1376256 | bytes 1720320 | tf_op jit(solution)/shard_map/convert_element_type | solution.py:152
  83.3 7.3 %collective-permute-start.9 = (bf16[32,1792]{1,0:T(8,128)(2,1)S(1)}, bf16[32,1792]{1,0:T(8,128)(2,1)S(1)}, u32[]{:S(2)}, u32[]{:S(2)}) collective-permute-start(bf16[32,1792]{1,0:T(8,128)(2,1)S(1)} %get-tuple-element.40), channel_id=1, source_target_pairs={{0,8},{4,0},{8,4},{1,9},{5,1},{9,5},{2,10},{6,2},{10,6},{3,11},{7,... | collective-permute-start | bytes 344072 | tf_op jit(solution)/shard_map/ppermute | solution.py:20
  90.6 2.5 %collective-permute-start.8 = (bf16[32,1792]{1,0:T(8,128)(2,1)S(1)}, bf16[32,1792]{1,0:T(8,128)(2,1)S(1)}, u32[]{:S(2)}, u32[]{:S(2)}) collective-permute-start(bf16[32,1792]{1,0:T(8,128)(2,1)S(1)} %get-tuple-element.41), channel_id=1, source_target_pairs={{0,4},{4,8},{8,0},{1,5},{5,9},{9,1},{2,6},{6,10},{10,2},{3,7},{7,1... | collective-permute-start | bytes 344072 | tf_op jit(solution)/shard_map/ppermute | solution.py:20
  93.1 0.0 copy-done.5
  93.1 0.0 copy-done.3
  93.1 0.0 copy-start.6
  93.1 0.0 copy-start.7
  93.1 2.4 %convolution_convert_fusion = bf16[1792,512]{1,0:T(8,128)(2,1)} fusion(bf16[384,1792]{1,0:T(8,128)(2,1)S(1)} %copy-done.3, bf16[384,512]{1,0:T(8,128)(2,1)S(1)} %copy-done.5), kind=kOutput, calls=%fused_computation | convolution fusion | flops 705560576 | bytes 3604480 | tf_op jit(solution)/shard_map/dot_general | solution.py:173
  95.5 6.4 %collective-permute-done.9 = bf16[32,1792]{1,0:T(8,128)(2,1)S(1)} collective-permute-done((bf16[32,1792]{1,0:T(8,128)(2,1)S(1)}, bf16[32,1792]{1,0:T(8,128)(2,1)S(1)}, u32[]{:S(2)}, u32[]{:S(2)}) %collective-permute-start.9) | collective-permute-done | bytes 114720 | tf_op jit(solution)/shard_map/ppermute | solution.py:20
  101.9 1.6 %collective-permute-done.8 = bf16[32,1792]{1,0:T(8,128)(2,1)S(1)} collective-permute-done((bf16[32,1792]{1,0:T(8,128)(2,1)S(1)}, bf16[32,1792]{1,0:T(8,128)(2,1)S(1)}, u32[]{:S(2)}, u32[]{:S(2)}) %collective-permute-start.8) | collective-permute-done | bytes 114720 | tf_op jit(solution)/shard_map/ppermute | solution.py:20
  103.5 0.0 copy-done.6
  103.5 0.0 copy-done.7
  103.5 0.8 multiply_convert_fusion
  104.4 0.0 all-to-all-done.1.columns
  104.4 1.3 %shard_map.78 = bf16[32,6144]{1,0:T(8,128)(2,1)} custom-call(s32[2]{0:T(128)S(1)} %pad_add_fusion.place, bf16[12,32,512]{2,1,0:T(8,128)(2,1)S(1)} %all-to-all-done.1.columns), custom_call_target="tpu_custom_call" | custom-call | bytes 1048576 | tf_op jit(solution)/shard_map/pallas_call | solution.py:40
  (4 shorter events, 0.0 us)
Async XLA Ops:
  0.6 55.9 %copy-start = (bf16[1792,512]{1,0:T(8,128)(2,1)S(1)}, bf16[1792,512]{1,0:T(8,128)(2,1)}, u32[]{:S(2)}) copy-start(bf16[1792,512]{1,0:T(8,128)(2,1)} %weight.3) | copy-start | bytes 5505028
  1.8 18.9 %collective-permute-start.1 = (bf16[32,1792]{1,0:T(8,128)(2,1)S(1)}, bf16[32,1792]{1,0:T(8,128)(2,1)S(1)}, u32[]{:S(2)}, u32[]{:S(2)}) collective-permute-start(bf16[32,1792]{1,0:T(8,128)(2,1)S(1)} %fusion), channel_id=1, source_target_pairs={{0,4},{4,8},{8,0},{1,5},{5,9},{9,1},{2,6},{6,10},{10,2},{3,7},{7,1... | collective-permute-start | bytes 344072 | tf_op jit(solution)/shard_map/ppermute | solution.py:20
  12.7 17.3 %collective-permute-start = (bf16[32,1792]{1,0:T(8,128)(2,1)S(1)}, bf16[32,1792]{1,0:T(8,128)(2,1)S(1)}, u32[]{:S(2)}, u32[]{:S(2)}) collective-permute-start(bf16[32,1792]{1,0:T(8,128)(2,1)S(1)} %fusion), channel_id=1, source_target_pairs={{0,8},{4,0},{8,4},{1,9},{5,1},{9,5},{2,10},{6,2},{10,6},{3,11},{7,... | collective-permute-start | bytes 344072 | tf_op jit(solution)/shard_map/ppermute | solution.py:20
  18.4 1.0 copy-start.1
  30.0 26.5 %all-to-all-start = ((bf16[12,32,512]{2,1,0:T(8,128)(2,1)}), bf16[12,32,512]{2,1,0:T(8,128)(2,1)S(1)}, u32[]{:S(2)}, u32[]{:S(2)}) async-start(bf16[12,32,512]{2,1,0:T(8,128)(2,1)} %shard_map.75), calls=%async_computation | async-start | bytes 786432 | tf_op jit(solution)/shard_map/all_to_all | solution.py:28
  41.4 24.2 %collective-permute-start.4 = (bf16[96,1792]{1,0:T(8,128)(2,1)S(1)}, bf16[96,1792]{1,0:T(8,128)(2,1)S(1)}, u32[]{:S(2)}, u32[]{:S(2)}) collective-permute-start(bf16[96,1792]{1,0:T(8,128)(2,1)S(1)} %constant_dynamic-update-slice_fusion.own), channel_id=1, source_target_pairs={{0,1},{1,2},{2,3},{3,0},{4,5},{5,6},{6,7},{7,4},{8,9},{9,10},{10,1... | collective-permute-start | bytes 1032200 | tf_op jit(solution)/shard_map/ppermute | solution.py:20
  43.4 25.6 %collective-permute-start.3 = (bf16[96,1792]{1,0:T(8,128)(2,1)S(1)}, bf16[96,1792]{1,0:T(8,128)(2,1)}, u32[]{:S(2)}, u32[]{:S(2)}) collective-permute-start(bf16[96,1792]{1,0:T(8,128)(2,1)S(1)} %constant_dynamic-update-slice_fusion.own), channel_id=1, source_target_pairs={{0,2},{1,3},{2,0},{3,1},{4,6},{5,7},{6,4},{7,5},{8,10},{9,11},{10,... | collective-permute-start | bytes 1032200 | tf_op jit(solution)/shard_map/ppermute | solution.py:20
  48.2 20.8 %collective-permute-start.2 = (bf16[96,1792]{1,0:T(8,128)(2,1)S(1)}, bf16[96,1792]{1,0:T(8,128)(2,1)}, u32[]{:S(2)}, u32[]{:S(2)}) collective-permute-start(bf16[96,1792]{1,0:T(8,128)(2,1)S(1)} %constant_dynamic-update-slice_fusion.own), channel_id=1, source_target_pairs={{0,3},{1,0},{2,1},{3,2},{4,7},{5,4},{6,5},{7,6},{8,11},{9,8},{10,9... | collective-permute-start | bytes 1032200 | tf_op jit(solution)/shard_map/ppermute | solution.py:20
  59.2 0.7 copy-start.4
  59.9 21.9 %collective-permute-start.5 = (bf16[96,1792]{1,0:T(8,128)(2,1)}, bf16[96,1792]{1,0:T(8,128)(2,1)}, u32[]{:S(2)}, u32[]{:S(2)}) collective-permute-start(bf16[96,1792]{1,0:T(8,128)(2,1)} %get-tuple-element.32), channel_id=1, source_target_pairs={{0,1},{1,2},{2,3},{3,0},{4,5},{5,6},{6,7},{7,4},{8,9},{9,10},{10,1... | collective-permute-start | bytes 1032200 | tf_op jit(solution)/shard_map/ppermute | solution.py:20
  63.7 18.1 %collective-permute-start.6 = (bf16[96,1792]{1,0:T(8,128)(2,1)}, bf16[96,1792]{1,0:T(8,128)(2,1)}, u32[]{:S(2)}, u32[]{:S(2)}) collective-permute-start(bf16[96,1792]{1,0:T(8,128)(2,1)} %get-tuple-element.33), channel_id=1, source_target_pairs={{0,2},{1,3},{2,0},{3,1},{4,6},{5,7},{6,4},{7,5},{8,10},{9,11},{10,... | collective-permute-start | bytes 1032200 | tf_op jit(solution)/shard_map/ppermute | solution.py:20
  65.7 16.2 %collective-permute-start.7 = (bf16[96,1792]{1,0:T(8,128)(2,1)}, bf16[96,1792]{1,0:T(8,128)(2,1)}, u32[]{:S(2)}, u32[]{:S(2)}) collective-permute-start(bf16[96,1792]{1,0:T(8,128)(2,1)} %get-tuple-element.34), channel_id=1, source_target_pairs={{0,3},{1,0},{2,1},{3,2},{4,7},{5,4},{6,5},{7,6},{8,11},{9,8},{10,9... | collective-permute-start | bytes 1032200 | tf_op jit(solution)/shard_map/ppermute | solution.py:20
  72.6 1.1 %copy-start.2 = (bf16[384,1792]{1,0:T(8,128)(2,1)}, bf16[384,1792]{1,0:T(8,128)(2,1)S(1)}, u32[]{:S(2)}) copy-start(bf16[384,1792]{1,0:T(8,128)(2,1)S(1)} %get-tuple-element.38) | copy-start | bytes 4128772
  73.7 19.4 %copy-start.5 = (bf16[384,512]{1,0:T(8,128)(2,1)S(1)}, bf16[384,512]{1,0:T(8,128)(2,1)}, u32[]{:S(2)}) copy-start(bf16[384,512]{1,0:T(8,128)(2,1)} %copy-done.4) | copy-start | bytes 1179652
  73.7 19.4 %copy-start.3 = (bf16[384,1792]{1,0:T(8,128)(2,1)S(1)}, bf16[384,1792]{1,0:T(8,128)(2,1)}, u32[]{:S(2)}) copy-start(bf16[384,1792]{1,0:T(8,128)(2,1)} %copy-done.2) | copy-start | bytes 4128772
  73.7 30.7 %all-to-all-start.1 = ((bf16[12,32,512]{2,1,0:T(8,128)(2,1)}), bf16[12,32,512]{2,1,0:T(8,128)(2,1)S(1)}, u32[]{:S(2)}, u32[]{:S(2)}) async-start(bf16[12,32,512]{2,1,0:T(8,128)(2,1)} %get-tuple-element.31), calls=%async_computation.1 | async-start | bytes 786432 | tf_op jit(solution)/shard_map/all_to_all | solution.py:28
  83.3 18.6 %collective-permute-start.9 = (bf16[32,1792]{1,0:T(8,128)(2,1)S(1)}, bf16[32,1792]{1,0:T(8,128)(2,1)S(1)}, u32[]{:S(2)}, u32[]{:S(2)}) collective-permute-start(bf16[32,1792]{1,0:T(8,128)(2,1)S(1)} %get-tuple-element.40), channel_id=1, source_target_pairs={{0,8},{4,0},{8,4},{1,9},{5,1},{9,5},{2,10},{6,2},{10,6},{3,11},{7,... | collective-permute-start | bytes 344072 | tf_op jit(solution)/shard_map/ppermute | solution.py:20
  90.6 12.9 %collective-permute-start.8 = (bf16[32,1792]{1,0:T(8,128)(2,1)S(1)}, bf16[32,1792]{1,0:T(8,128)(2,1)S(1)}, u32[]{:S(2)}, u32[]{:S(2)}) collective-permute-start(bf16[32,1792]{1,0:T(8,128)(2,1)S(1)} %get-tuple-element.41), channel_id=1, source_target_pairs={{0,4},{4,8},{8,0},{1,5},{5,9},{9,1},{2,6},{6,10},{10,2},{3,7},{7,1... | collective-permute-start | bytes 344072 | tf_op jit(solution)/shard_map/ppermute | solution.py:20
  93.1 10.4 %copy-start.6 = (bf16[32,1792]{1,0:T(8,128)(2,1)S(1)}, bf16[32,1792]{1,0:T(8,128)(2,1)}, u32[]{:S(2)}) copy-start(bf16[32,1792]{1,0:T(8,128)(2,1)} %param.5) | copy-start | bytes 344068
  93.1 10.4 %copy-start.7 = (bf16[32,1792]{1,0:T(8,128)(2,1)S(1)}, bf16[32,1792]{1,0:T(8,128)(2,1)}, u32[]{:S(2)}) copy-start(bf16[32,1792]{1,0:T(8,128)(2,1)} %param.4) | copy-start | bytes 344068
